TPU v7x, 32 devices: a whole 2x2x4 slice. The times are simulated.
32 devices in a mesh: region: 2 (over x), inner: 16 (over z, y, core).
Axes of the slice: x: 2, y: 2, z: 4, core: 2. Of those that a mesh axis runs over, the one named last changes fastest.
Arguments:
- density: float32 [6, 48, 144], P('region', 'inner'), may hold values from 0.8 to 1.2
- momentum: float32 [3, 6, 48, 144], P(None, 'region', 'inner'), may hold values from -1 to 1
- energy: float32 [6, 48, 144], P('region', 'inner'), may hold values from 4 to 5
- fuel_density: float32 [6, 48, 144], P('region', 'inner'), may hold values from 0.02 to 0.2
- drop_pos: float32 [3, 65536], P(None, ('region', 'inner')), may hold values from -1 to 1
- drop_vel: float32 [3, 65536], P(None, ('region', 'inner')), may hold values from -3 to 3
- drop_mass: float32 [65536], P(('region', 'inner')), may hold values from 0.5 to 2
- block_cell: int32 [2048], P(('region', 'inner')), may hold values from 0 to 767, as said below
- block_count: int32 [2048], P(('region', 'inner')), may hold values from 1 to 32, as said below
Outputs:
- gas_state: float32 [6, 6, 48, 144], P(None, 'region', 'inner')
- drop_vel_out: float32 [3, 65536], P(None, ('region', 'inner'))
- drop_mass_out: float32 [65536], P(('region', 'inner'))
Inputs may be any that keep to these rules, and one draw needn't show every extreme that they name: `block_cell`: within the 64 blocks of one device the ids never fall. With owner = id // 48, at most 8 blocks of one device lie on the hexahedra of one owner; on every device some owner has exactly 8, and in every region one owner has exactly 8 from every device of the region. `block_count`: every device has a block with 32 live droplets.
All inputs are finite; a program needn't handle non-finite values.
Results may differ from a plain program's by a relative error of at most 0.00005.
Values sent between devices are 32-bit elements; how exact they have to be, the bound alone decides.
A program may use at most 64 MiB of HBM per device.

v0:
```python
import jax
import jax.numpy as jnp
from jax import lax
from jax.sharding import PartitionSpec as P

PB = 32


GAMMA = 1.4
TIME_STEP = 0.05
EVAP_RATE = 0.5
LATENT = 0.5
END_WEIGHT = 1.0 / 3.0


def padded_2(block, sides, width):
    for axis, dim in sides:
        count = lax.axis_size(axis)
        forward = [(i, i + 1) for i in range(count - 1)]
        forward.append((count - 1, 0))
        backward = [(target, source) for source, target in forward]
        low = lax.ppermute(
            lax.slice_in_dim(block, block.shape[dim] - width, None, axis=dim), axis, forward
        )
        high = lax.ppermute(lax.slice_in_dim(block, 0, width, axis=dim), axis, backward)
        block = jnp.concatenate([low, block, high], axis=dim)
    return block


def derivative_matrix():
    return jnp.array([[-1.5, 2.0, -0.5], [-0.5, 0.0, 0.5], [0.5, -2.0, 1.5]], jnp.float32)


def node_weights():
    gll_line = jnp.array([1.0 / 3.0, 4.0 / 3.0, 1.0 / 3.0], jnp.float32)
    return (gll_line[:, None, None] * gll_line[None, :, None] * gll_line[None, None, :]).reshape(27)


def euler_flux(conserved, direction):
    pressure_node = (GAMMA - 1.0) * (
        conserved[4]
        - 0.5 * (conserved[1] ** 2 + conserved[2] ** 2 + conserved[3] ** 2) / conserved[0]
    )
    normal_speed = conserved[1 + direction] / conserved[0]
    flux_rows = [conserved[1 + direction]]
    for component in range(3):
        momentum_flux = conserved[1 + component] * normal_speed
        if component == direction:
            momentum_flux = momentum_flux + pressure_node
        flux_rows.append(momentum_flux)
    flux_rows.append((conserved[4] + pressure_node) * normal_speed)
    flux_rows.append(conserved[5] * normal_speed)
    return (jnp.stack(flux_rows), normal_speed, pressure_node)


def face_flux(state_left, state_right, direction):
    flux_left, speed_left, pressure_left = euler_flux(state_left, direction)
    flux_right, speed_right, pressure_right = euler_flux(state_right, direction)
    wave_left = jnp.abs(speed_left) + jnp.sqrt(GAMMA * pressure_left / state_left[0])
    wave_right = jnp.abs(speed_right) + jnp.sqrt(GAMMA * pressure_right / state_right[0])
    wave_speed = jnp.maximum(wave_left, wave_right)
    return 0.5 * (flux_left + flux_right) - 0.5 * wave_speed * (state_right - state_left)


def axis_tendency(padded, along_axis, direction):
    shifted_axes = jnp.moveaxis(padded, along_axis, -1)
    length = shifted_axes.shape[-1] - 2
    elements = length // 3
    interior = shifted_axes[..., 1:-1]
    flux_nodes, unused_speed, unused_pressure = euler_flux(interior, direction)
    grouped = flux_nodes.reshape(flux_nodes.shape[:-1] + (elements, 3))
    volume = jnp.einsum(
        "...j,ij->...i", grouped, derivative_matrix(), precision=lax.Precision.HIGHEST
    )
    outer_left = shifted_axes[..., 0 : length + 1 : 3]
    outer_right = shifted_axes[..., 1 : length + 2 : 3]
    face_values = face_flux(outer_left, outer_right, direction)
    lift_first = -(face_values[..., :-1] - grouped[..., 0]) / END_WEIGHT
    lift_last = (face_values[..., 1:] - grouped[..., 2]) / END_WEIGHT
    lifted = jnp.stack([lift_first, jnp.zeros_like(lift_first), lift_last], -1)
    result = -(volume + lifted)
    return jnp.moveaxis(result.reshape(result.shape[:-2] + (length,)), -1, along_axis)


def fluid_tendency(conserved):
    rimmed = padded_2(conserved, (("region", 1), ("inner", 2)), 1)
    along_x = axis_tendency(rimmed[:, :, 1:-1, :], 1, 0)
    along_y = axis_tendency(rimmed[:, 1:-1, :, :], 2, 1)
    along_z = axis_tendency(jnp.pad(conserved, ((0, 0), (0, 0), (0, 0), (1, 1)), mode="wrap"), 3, 2)
    return along_x + along_y + along_z


def lagrange_weights(positions):
    basis_values = jnp.stack(
        [
            0.5 * positions * (positions - 1.0),
            1.0 - positions * positions,
            0.5 * positions * (positions + 1.0),
        ]
    )
    weights = (
        basis_values[:, None, None, 0]
        * basis_values[None, :, None, 1]
        * basis_values[None, None, :, 2]
    )
    return weights.reshape((27,) + positions.shape[1:])


def droplet_terms(block_states, weights, velocity, droplet_mass, live_slots, parcel):
    gas_values = jnp.einsum("bfk,kbp->fbp", block_states, weights, precision=lax.Precision.HIGHEST)
    relative = gas_values[1:4] / gas_values[0] - velocity
    fuel_share = gas_values[5] / gas_values[0]
    cube_root = jnp.exp(jnp.log(droplet_mass) / 3.0)
    acceleration = live_slots * relative / (cube_root * cube_root)
    evaporation = (
        live_slots
        * EVAP_RATE
        * cube_root
        * jnp.sqrt(1.0 + jnp.sum(relative * relative, 0))
        * (1.0 - fuel_share)
    )
    drag_force = droplet_mass * acceleration
    sources = jnp.stack(
        [
            evaporation,
            evaporation * velocity[0] - drag_force[0],
            evaporation * velocity[1] - drag_force[1],
            evaporation * velocity[2] - drag_force[2],
            evaporation * (LATENT + 0.5 * jnp.sum(velocity * velocity, 0))
            - jnp.sum(drag_force * velocity, 0),
            evaporation,
        ]
    )
    deposit = (
        jnp.einsum("kbp,fbp->bfk", weights, sources, precision=lax.Precision.HIGHEST)
        / node_weights()
        * parcel
    )
    return (deposit, acceleration, -evaporation)


def element_rows(conserved):
    elements = conserved.shape[3] // 3
    return conserved.reshape(6, 3, 3, elements, 3).transpose(3, 0, 1, 2, 4).reshape(elements, 162)


def node_layout(rows_table):
    elements = rows_table.shape[0]
    return (
        rows_table.reshape(elements, 6, 3, 3, 3)
        .transpose(1, 2, 3, 0, 4)
        .reshape(6, 3, 3, 3 * elements)
    )


def on_device(
    density, momentum, energy, fuel_density, drop_pos, drop_vel, drop_mass, block_cell, block_count
):
    conserved = jnp.concatenate([density[None], momentum, energy[None], fuel_density[None]], 0)
    elements = conserved.shape[3] // 3
    blocks = block_cell.shape[0]
    parcel = 4.0 * elements / (blocks * PB)
    weights = lagrange_weights(drop_pos.reshape(3, blocks, PB))
    velocity = drop_vel.reshape(3, blocks, PB)
    droplet_mass = drop_mass.reshape(blocks, PB)
    live_slots = (jnp.arange(PB)[None, :] < block_count[:, None]).astype(jnp.float32)

    def fetch_states(rows_table):
        shard_rows = lax.all_gather(rows_table, "inner", axis=0, tiled=True)
        chosen = (
            block_cell[:, None] == jnp.arange(shard_rows.shape[0], dtype=jnp.int32)[None, :]
        ).astype(jnp.float32)
        return jnp.dot(
            chosen, shard_rows, precision=lax.Precision.HIGHEST, preferred_element_type=jnp.float32
        )

    def return_sources(deposit_rows):
        chosen = (
            jnp.arange(lax.axis_size("inner") * elements, dtype=jnp.int32)[:, None]
            == block_cell[None, :]
        ).astype(jnp.float32)
        return lax.psum_scatter(
            jnp.dot(
                chosen,
                deposit_rows,
                precision=lax.Precision.HIGHEST,
                preferred_element_type=jnp.float32,
            ),
            "inner",
            scatter_dimension=0,
            tiled=True,
        )

    def section_rates(fields_now, velocity_now, mass_now):
        block_states = fetch_states(element_rows(fields_now)).reshape(blocks, 6, 27)
        deposit, acceleration, mass_rate = droplet_terms(
            block_states, weights, velocity_now, mass_now, live_slots, parcel
        )
        summed = return_sources(deposit.reshape(blocks, 162))
        return (fluid_tendency(fields_now) + node_layout(summed), acceleration, mass_rate)

    rate_first, accel_first, shrink_first = section_rates(conserved, velocity, droplet_mass)
    fields_one = conserved + TIME_STEP * rate_first
    velocity_one = velocity + TIME_STEP * accel_first
    mass_one = droplet_mass + TIME_STEP * shrink_first
    rate_second, accel_second, shrink_second = section_rates(fields_one, velocity_one, mass_one)
    gas_state = 0.5 * conserved + 0.5 * (fields_one + TIME_STEP * rate_second)
    velocity_two = 0.5 * velocity + 0.5 * (velocity_one + TIME_STEP * accel_second)
    mass_two = 0.5 * droplet_mass + 0.5 * (mass_one + TIME_STEP * shrink_second)
    return (gas_state, velocity_two.reshape(3, -1), mass_two.reshape(-1))


def solution(mesh):
    placed = (
        P("region", "inner", None),
        P(None, "region", "inner", None),
        P("region", "inner", None),
        P("region", "inner", None),
        P(None, ("region", "inner")),
        P(None, ("region", "inner")),
        P(("region", "inner")),
        P(("region", "inner")),
        P(("region", "inner")),
    )
    return jax.shard_map(
        on_device,
        mesh=mesh,
        in_specs=placed,
        out_specs=(
            P(None, "region", "inner", None),
            P(None, ("region", "inner")),
            P(("region", "inner")),
        ),
        check_vma=False,
    )
```

profile of v0, /device:TPU:0, one launch (start us, length us, event | category | flops | bytes accessed | tf_op | source)
XLA Modules:
  0.0 198.5 jit_solution(14710807144908215036)
XLA Ops:
  7.2 0.8 reshape.613
  8.8 0.9 reshape.616
  9.7 0.9 slice_reduce_fusion
  10.7 0.8 multiply_reduce_fusion.5
  11.6 0.8 add_multiply_fusion.2
  13.1 0.9 copy.550
  16.0 25.5 %all_gather.6 = f32[768,162]{1,0:T(8,128)S(1)} all-gather(f32[48,162]{1,0:T(8,128)S(1)} %copy.548), channel_id=1, replica_groups=mesh['region'=2,'inner'=16] {'inner'}, dimensions={0}, use_global_device_ids=true | all-gather | bytes 528768 | tf_op jit(solution)/shard_map/all_gather | solution.py:169
  41.5 0.8 fusion.5
  42.5 1.0 fusion.128
  44.9 1.8 fusion.1
  46.8 1.4 fusion.3
  48.4 1.6 collective-permute-start.1
  58.8 4.7 %collective-permute-done.2 = f32[6,5,1,144]{3,0,2,1:T(8,128)S(1)} collective-permute-done((f32[6,5,1,144]{3,0,2,1:T(8,128)S(1)}, f32[6,5,1,144]{3,0,2,1:T(8,128)S(1)}, u32[]{:S(2)}, u32[]{:S(2)}) %collective-permute-start.2) | collective-permute-done | bytes 17312 | tf_op jit(solution)/shard_map/ppermute | solution.py:22
  64.6 37.7 %reduce-scatter.3.cloned.1.call-done = f32[48,162]{1,0:T(8,128)} async-done(((f32[768,162]{1,0:T(8,128)}), f32[48,162]{1,0:T(8,128)}) %reduce-scatter.3.cloned.1.call-update) | async-done | bytes 31120 | tf_op jit(solution)/shard_map/reduce_scatter | solution.py:182
  102.3 0.9 copy.564
  107.5 21.5 %all_gather.7 = f32[768,162]{1,0:T(8,128)S(1)} all-gather(f32[48,162]{1,0:T(8,128)S(1)} %copy.591), channel_id=1, replica_groups=mesh['region'=2,'inner'=16] {'inner'}, dimensions={0}, use_global_device_ids=true | all-gather | bytes 528768 | tf_op jit(solution)/shard_map/all_gather | solution.py:169
  129.0 0.8 fusion.4
  130.0 1.0 fusion.129
  131.5 1.8 fusion
  133.4 1.4 fusion.2
  137.7 1.6 collective-permute-start.5
  145.2 4.7 %collective-permute-done.6 = f32[6,5,1,144]{3,0,2,1:T(8,128)S(1)} collective-permute-done((f32[6,5,1,144]{3,0,2,1:T(8,128)S(1)}, f32[6,5,1,144]{3,0,2,1:T(8,128)S(1)}, u32[]{:S(2)}, u32[]{:S(2)}) %collective-permute-start.6) | collective-permute-done | bytes 17312 | tf_op jit(solution)/shard_map/ppermute | solution.py:22
  150.9 37.9 %reduce-scatter.5.cloned.1.call-done = f32[48,162]{1,0:T(8,128)} async-done(((f32[768,162]{1,0:T(8,128)}), f32[48,162]{1,0:T(8,128)}) %reduce-scatter.5.cloned.1.call-update) | async-done | bytes 31120 | tf_op jit(solution)/shard_map/reduce_scatter | solution.py:182
  188.8 0.9 copy.600
  (278 shorter events, 31.1 us)
Async XLA Ops:
  7.2 95.1 %reduce-scatter.3.cloned.1.call-start = ((), (), s32[]{:S(2)}) async-start(), calls=%async_computation.2 | async-start | bytes 835584 | tf_op jit(solution)/shard_map/reduce_scatter | solution.py:182
  12.8 1.2 copy-start.3
  13.1 1.3 copy-start.2
  13.1 1.6 copy-start
  14.1 1.4 copy-start.1
  15.1 26.4 %copy-start.7 = (s32[64]{0:T(128)S(1)}, s32[64]{0:T(128)}, u32[]{:S(2)}) copy-start(s32[64]{0:T(128)} %param.24) | copy-start | bytes 772
  42.3 1.4 copy-start.8
  43.5 1.2 copy-start.9
  46.8 5.5 %slice-start = ((f32[3,3,3,144]{3,2,1,0:T(4,128)}), f32[1,3,3,144]{3,2,1,0:T(4,128)S(1)}, s32[]{:S(2)}) async-start(f32[3,3,3,144]{3,2,1,0:T(4,128)} %param.18), calls=%async_computation.4 | async-start | bytes 24576 | tf_op jit(solution)/shard_map/slice | solution.py:45
  48.2 140.6 %reduce-scatter.5.cloned.1.call-start = ((), (), s32[]{:S(2)}) async-start(), calls=%async_computation.3 | async-start | bytes 835584 | tf_op jit(solution)/shard_map/reduce_scatter | solution.py:182
  48.4 8.3 %collective-permute-start.1 = (f32[6,1,3,144]{3,0,2,1:T(8,128)S(1)}, f32[6,1,3,144]{3,0,2,1:T(8,128)S(1)}, u32[]{:S(2)}, u32[]{:S(2)}) collective-permute-start(f32[6,1,3,144]{3,0,2,1:T(8,128)S(1)} %get-tuple-element.149), channel_id=1, source_target_pairs={{16,0},{0,16},{17,1},{1,17},{18,2},{2,18},{19,3},{3,19},{20,4},{4,... | collective-permute-start | bytes 31112 | tf_op jit(solution)/shard_map/ppermute | solution.py:25
  50.0 6.8 %collective-permute-start = (f32[6,1,3,144]{3,0,2,1:T(8,128)S(1)}, f32[6,1,3,144]{3,0,2,1:T(8,128)S(1)}, u32[]{:S(2)}, u32[]{:S(2)}) collective-permute-start(f32[6,1,3,144]{3,0,2,1:T(8,128)S(1)} %get-tuple-element.148), channel_id=1, source_target_pairs={{0,16},{16,0},{1,17},{17,1},{2,18},{18,2},{3,19},{19,3},{4,20},{20... | collective-permute-start | bytes 31112 | tf_op jit(solution)/shard_map/ppermute | solution.py:22
  53.2 1.6 copy-start.6
  55.6 2.1 %copy-start.5 = (f32[3,3,1,1]{1,0,3,2:T(4,128)S(1)}, f32[3,3,1,1]{1,0,3,2:T(4,128)}, u32[]{:S(2)}) copy-start(f32[3,3,1,1]{1,0,3,2:T(4,128)} %constant.75) | copy-start | bytes 112
  57.1 1.7 collective-permute-start.3
  57.2 6.4 %collective-permute-start.2 = (f32[6,5,1,144]{3,0,2,1:T(8,128)S(1)}, f32[6,5,1,144]{3,0,2,1:T(8,128)S(1)}, u32[]{:S(2)}, u32[]{:S(2)}) collective-permute-start(f32[6,5,1,144]{3,0,2,1:T(8,128)S(1)} %get-tuple-element.132), channel_id=1, source_target_pairs={{0,1},{1,2},{2,3},{3,4},{4,5},{5,6},{6,7},{7,8},{8,9},{9,10},{10,1... | collective-permute-start | bytes 51848 | tf_op jit(solution)/shard_map/ppermute | solution.py:22
  136.2 3.9 %copy-start.4 = (f32[2048]{0:T(1024)S(1)}, f32[2048]{0:T(1024)}, u32[]{:S(2)}) copy-start(f32[2048]{0:T(1024)} %param.23) | copy-start | bytes 24580
  137.7 5.0 %collective-permute-start.5 = (f32[6,1,3,144]{3,0,2,1:T(8,128)S(1)}, f32[6,1,3,144]{3,0,2,1:T(8,128)S(1)}, u32[]{:S(2)}, u32[]{:S(2)}) collective-permute-start(f32[6,1,3,144]{3,0,2,1:T(8,128)S(1)} %get-tuple-element.143), channel_id=1, source_target_pairs={{16,0},{0,16},{17,1},{1,17},{18,2},{2,18},{19,3},{3,19},{20,4},{4,... | collective-permute-start | bytes 31112 | tf_op jit(solution)/shard_map/ppermute | solution.py:25
  139.3 3.8 %collective-permute-start.4 = (f32[6,1,3,144]{3,0,2,1:T(8,128)S(1)}, f32[6,1,3,144]{3,0,2,1:T(8,128)S(1)}, u32[]{:S(2)}, u32[]{:S(2)}) collective-permute-start(f32[6,1,3,144]{3,0,2,1:T(8,128)S(1)} %get-tuple-element.142), channel_id=1, source_target_pairs={{0,16},{16,0},{1,17},{17,1},{2,18},{18,2},{3,19},{19,3},{4,20},{20... | collective-permute-start | bytes 31112 | tf_op jit(solution)/shard_map/ppermute | solution.py:22
  143.5 1.7 collective-permute-start.7
  143.5 6.4 %collective-permute-start.6 = (f32[6,5,1,144]{3,0,2,1:T(8,128)S(1)}, f32[6,5,1,144]{3,0,2,1:T(8,128)S(1)}, u32[]{:S(2)}, u32[]{:S(2)}) collective-permute-start(f32[6,5,1,144]{3,0,2,1:T(8,128)S(1)} %get-tuple-element.114), channel_id=1, source_target_pairs={{0,1},{1,2},{2,3},{3,4},{4,5},{5,6},{6,7},{7,8},{8,9},{9,10},{10,1... | collective-permute-start | bytes 51848 | tf_op jit(solution)/shard_map/ppermute | solution.py:22
Sparse Core Ops, SparseCore 0:
  48.3 53.8 reduce-scatter.2
  134.9 53.8 reduce-scatter.4
where the time goes:
time: 199 us; the launch traced here: 198 us
  waiting for transfers between devices  86.6 us (44%)
  blocking collectives  47 us (24%)
  local copies, waits for them, and re-layouts  26.8 us (13%)
  between operations  15.4 us (8%)
  matrix products  11.6 us (6%)
  other arithmetic  5.71 us (3%)
  starting transfers between devices  5.34 us (3%)
    reduce_scatter x2, waiting for transfers between devices, return_sources(): lax.psum_scatter(jnp.dot(chosen, deposit_rows, precision=lax.Precision.HI...  75.6 us
    all_gather x2, blocking collectives, fetch_states(): shard_rows = lax.all_gather(rows_table, 'inner', axis=0, tiled=True)  47 us
    ppermute x4, waiting for transfers between devices, padded_2(): lax.ppermute(lax.slice_in_dim(block, block.shape[dim] - width, None, axis...  9.85 us
    another operation x42, local copies, waits for them, and re-layouts, euler_flux(): return (jnp.stack(flux_rows), normal_speed, pressure_node)  4.98 us
  transfers between devices with their start and end apart: 10, of which 7 were waited for; matrix products, arithmetic and copies ran while one was open for 8% of the time, Pallas kernels for 0%

commit v1 on v0

v1 whole, which is shorter than its diff:
```python
import functools

import jax
import jax.numpy as jnp
import numpy as np
from jax import lax
from jax.experimental import pallas as pl
from jax.experimental.pallas import tpu as pltpu
from jax.sharding import PartitionSpec as P

PB = 32
CAP = 8
GAMMA = 1.4
TIME_STEP = 0.05
EVAP_RATE = 0.5
LATENT = 0.5
LANES = 128
NODES = 32
SENT = 5 * NODES
WIDE = 256
STRIDES = (3, 1, 9)
F32, BF16 = jnp.float32, jnp.bfloat16
MESH = pl.DeviceIdType.MESH


def derivative_rows():
    line = np.array([[-1.5, 2.0, -0.5], [-0.5, 0.0, 0.5], [0.5, -2.0, 1.5]])
    table = np.zeros((NODES, 3 * NODES))
    for node in range(27):
        for d, stride in enumerate(STRIDES):
            place = node // stride % 3
            for j in range(3):
                table[node, d * NODES + node + (j - place) * stride] = -line[place, j]
    return np.concatenate([table, table], 1).astype(np.float32)


def node_scale():
    q = np.array([1.0 / 3.0, 4.0 / 3.0, 1.0 / 3.0])
    table = np.zeros((NODES, LANES), np.float32)
    for node in range(27):
        table[node] = 1.0 / (q[node // 3 % 3] * q[node % 3] * q[node // 9])
    return table


def halves(value):
    high = value.astype(BF16)
    return high, (value - high.astype(F32)).astype(BF16)


def nt_dot(left, right):
    return lax.dot_general(left, right, (((1,), (1,)), ((), ())), preferred_element_type=F32)


def field(value, f):
    return value[NODES * f : NODES * (f + 1)]


def flux_parts(value):
    inverse = 1.0 / field(value, 0)
    speeds = [field(value, 1 + c) * inverse for c in range(3)]
    kinetic = sum(field(value, 1 + c) * speeds[c] for c in range(3))
    pressure = (GAMMA - 1.0) * (field(value, 5) - 0.5 * kinetic)
    sound = jnp.sqrt(GAMMA * pressure * inverse)
    return speeds, pressure, sound


def flux_rows(value, parts, d):
    speeds, pressure, _ = parts
    speed = speeds[d]
    rows = [field(value, 1 + d)]
    for c in range(3):
        row = field(value, 1 + c) * speed
        rows.append(row + pressure if c == d else row)
    rows.append(field(value, 4) * speed)
    rows.append((field(value, 5) + pressure) * speed)
    return rows


def gas_kernel(
    elements, parcel,
    fields_ref, ids_ref, slot_ref, live_ref, pos_ref, vel_ref, mass_ref, deriv_ref, scale_ref,
    gas_out, vel_out, mass_out,
    fields_one, tend, flux_scr, weights, drop_hot, cell_hot,
    ids_in, states_out, states_in, dep_out, dep_in, low_in, high_in, dep_acc, vel_one, mass_one,
    ids_sems, state_sems, dep_sems, halo_send, halo_recv,
):
    n_inner, n_region = lax.axis_size("inner"), lax.axis_size("region")
    me, my_region = lax.axis_index("inner"), lax.axis_index("region")
    slots = n_inner * CAP
    drops = pos_ref.shape[1]
    chunk = min(512, drops)
    inner_low, inner_high = lax.rem(me + n_inner - 1, n_inner), lax.rem(me + 1, n_inner)
    region_low = lax.rem(my_region + n_region - 1, n_region)
    region_high = lax.rem(my_region + 1, n_region)

    def peer_of(j):
        return lax.rem(me + j, n_inner)

    barrier = pltpu.get_barrier_semaphore()

    @pl.loop(1, n_inner)
    def _(j):
        pl.semaphore_signal(barrier, inc=1, device_id=(my_region, peer_of(j)), device_id_type=MESH)

    region_peers = [region_high] if n_region == 2 else [region_low, region_high]
    for other in region_peers:
        pl.semaphore_signal(barrier, inc=1, device_id=(other, me), device_id_type=MESH)

    row = lax.broadcasted_iota(jnp.int32, (NODES, drops), 0)

    def basis(d, place):
        t = pos_ref[d : d + 1, :]
        first, mid, last = 0.5 * t * (t - 1.0), 1.0 - t * t, 0.5 * t * (t + 1.0)
        return jnp.where(place == 0, first, jnp.where(place == 1, mid, last))

    product = basis(0, row // 3 % 3) * basis(1, row % 3) * basis(2, row // 9)
    weights[...] = jnp.where(row < 27, product, 0.0)
    hot_row = lax.broadcasted_iota(jnp.int32, (slots, drops), 0).astype(F32)
    hot = (hot_row == slot_ref[0:1, :]).astype(F32).astype(BF16)
    drop_hot[0:slots, :] = hot
    drop_hot[slots : 2 * slots, :] = hot

    pl.semaphore_wait(barrier, n_inner - 1 + len(region_peers))

    def exchange(src, dst, sems):
        @pl.loop(1, n_inner)
        def _(j):
            peer = peer_of(j)
            pltpu.make_async_remote_copy(
                src_ref=src.at[peer], dst_ref=dst.at[me],
                send_sem=sems.at[0], recv_sem=sems.at[1],
                device_id=(my_region, peer), device_id_type=MESH,
            ).start()

    def whole(src, dst, sems):
        part = pl.ds(0, n_inner - 1)
        return pltpu.make_async_remote_copy(
            src_ref=src.at[part], dst_ref=dst.at[part],
            send_sem=sems.at[0], recv_sem=sems.at[1],
            device_id=(my_region, inner_high), device_id_type=MESH,
        )

    exchange(ids_ref, ids_in, ids_sems)
    ids_in[me] = ids_ref[me]

    lane = lax.broadcasted_iota(jnp.int32, (SENT, LANES), 1)
    node = lax.broadcasted_iota(jnp.int32, (6 * NODES, LANES), 0) % NODES

    def halo_copies(section, src):
        copies = [
            (src, high_in.at[section, 1], 0, (my_region, inner_low)),
            (src, low_in.at[section, 1], 1, (my_region, inner_high)),
            (src, high_in.at[section, 0], 2, (region_low, me)),
        ]
        if n_region != 2:
            copies.append((src, low_in.at[section, 0], 3, (region_high, me)))
        return [
            pltpu.make_async_remote_copy(
                src_ref=a, dst_ref=b, send_sem=halo_send.at[section, i],
                recv_sem=halo_recv.at[section, i], device_id=dev, device_id_type=MESH,
            )
            for a, b, i, dev in copies
        ]

    def lifts(value, parts, low, high, d):
        stride = STRIDES[d]
        place = node // stride % 3
        first, last = (place == 0) & (node < 27), (place == 2) & (node < 27)
        rows = 6 * NODES
        beyond = jnp.where(
            first, pltpu.roll(low, rows - 2 * stride, 0),
            jnp.where(last, pltpu.roll(high, 2 * stride, 0), value),
        )
        other = flux_parts(beyond)
        wave = 1.5 * jnp.maximum(
            jnp.abs(parts[0][d]) + parts[2], jnp.abs(other[0][d]) + other[2]
        )
        sign = jnp.where(first, 1.5, -1.5)[0:NODES]
        here, there = flux_rows(value, parts, d), flux_rows(beyond, other, d)
        return [
            sign * (there[f] - here[f]) + wave * (field(beyond, f) - field(value, f))
            for f in range(6)
        ]

    def section_rates(section, src, vel_src, mass_src, finish_drops):
        value = src[...]
        asked = jnp.where(lane < elements, value[0:SENT], 0.0)
        rows = nt_dot(cell_hot[...], jnp.concatenate(halves(asked), 1))
        states_out[section, :, :, 0:SENT] = rows.reshape(n_inner, CAP, SENT)
        exchange(states_out.at[section], states_in.at[section], state_sems.at[section])
        states_in[section, me] = states_out[section, me]
        halos = halo_copies(section, src)
        for copy in halos:
            copy.start()

        parts = flux_parts(value)
        for d in range(3):
            for f, part in enumerate(flux_rows(value, parts, d)):
                flux_scr[NODES * d : NODES * (d + 1), LANES * f : LANES * (f + 1)] = part
        volume = jnp.dot(
            deriv_ref[...].astype(BF16), jnp.concatenate(halves(flux_scr[...]), 0),
            preferred_element_type=F32,
        )
        along = lifts(value, parts, pltpu.roll(value, 1, 1), pltpu.roll(value, LANES - 1, 1), 2)
        for f in range(6):
            tend[NODES * f : NODES * (f + 1), :] = (
                volume[:, LANES * f : LANES * (f + 1)] + along[f]
            )

        whole(states_out.at[section], states_in.at[section], state_sems.at[section]).wait_recv()
        states = states_in[section].reshape(slots, WIDE).T[0:SENT]
        states_two = jnp.concatenate(halves(states), 1)
        dep_acc[...] = jnp.zeros_like(dep_acc)

        @pl.loop(0, drops // chunk)
        def _(i):
            at = pl.ds(pl.multiple_of(i * chunk, chunk), chunk)
            spread = jnp.dot(states_two, drop_hot[:, at], preferred_element_type=F32)
            w = weights[:, at]
            gas = [jnp.sum(field(spread, f) * w, 0, keepdims=True) for f in range(5)]
            inverse = 1.0 / gas[0]
            vel = [vel_src[c : c + 1, at] for c in range(3)]
            mass, live = mass_src[0:1, at], live_ref[0:1, at]
            rel = [gas[1 + c] * inverse - vel[c] for c in range(3)]
            cube_root = jnp.exp(jnp.log(mass) * (1.0 / 3.0))
            drag = live / (cube_root * cube_root)
            accel = [drag * rel[c] for c in range(3)]
            evap = (
                live * EVAP_RATE * cube_root
                * jnp.sqrt(1.0 + (rel[0] * rel[0] + rel[1] * rel[1] + rel[2] * rel[2]))
                * (1.0 - gas[4] * inverse)
            )
            force = [mass * accel[c] for c in range(3)]
            work = sum(force[c] * vel[c] for c in range(3))
            square = sum(vel[c] * vel[c] for c in range(3))
            sources = [evap] + [evap * vel[c] - force[c] for c in range(3)]
            sources.append(evap * (LATENT + 0.5 * square) - work)
            placed = jnp.concatenate([w * s for s in sources], 0)
            dep_acc[...] += nt_dot(jnp.concatenate(halves(placed), 0), drop_hot[0:slots, at])
            finish_drops(at, vel, mass, accel, evap)

        summed = dep_acc[0:SENT, :] + dep_acc[SENT : 2 * SENT, :]
        dep_out[section, :, :, 0:SENT] = summed.T.reshape(n_inner, CAP, SENT)
        exchange(dep_out.at[section], dep_in.at[section], dep_sems.at[section])
        dep_in[section, me] = dep_out[section, me]

        for copy in halos:
            copy.wait_recv()
        low_x = high_in[section, 0] if n_region == 2 else low_in[section, 0]
        along_x = lifts(value, parts, low_x, high_in[section, 0], 0)
        along_y = lifts(value, parts, low_in[section, 1], high_in[section, 1], 1)
        for f in range(6):
            tend[NODES * f : NODES * (f + 1), :] += along_x[f] + along_y[f]

        whole(dep_out.at[section], dep_in.at[section], dep_sems.at[section]).wait_recv()
        deposits = dep_in[section].reshape(slots, WIDE).T[0:SENT]
        arrived = jnp.dot(
            jnp.concatenate(halves(deposits), 0), cell_hot[:, 0:LANES], preferred_element_type=F32
        )
        arrived = arrived[0:SENT] + arrived[SENT : 2 * SENT]
        scale = scale_ref[...] * parcel
        rates = []
        for f, source in enumerate((0, 1, 2, 3, 0, 4)):
            rates.append(
                tend[NODES * f : NODES * (f + 1), :] + scale * field(arrived, source)
            )
        return value, rates, halos

    def drops_first(at, vel, mass, accel, evap):
        for c in range(3):
            vel_one[c : c + 1, at] = vel[c] + TIME_STEP * accel[c]
        mass_one[0:1, at] = mass - TIME_STEP * evap

    def drops_second(at, vel, mass, accel, evap):
        for c in range(3):
            vel_out[c : c + 1, at] = 0.5 * vel_ref[c : c + 1, at] + 0.5 * (
                vel[c] + TIME_STEP * accel[c]
            )
        mass_out[0:1, at] = 0.5 * mass_ref[0:1, at] + 0.5 * (mass - TIME_STEP * evap)

    whole(ids_ref, ids_in, ids_sems).wait_recv()
    lane_id = lax.broadcasted_iota(jnp.int32, (slots, LANES), 1).astype(F32)
    own = (ids_in[...].reshape(slots, LANES) == element_of(lane_id, elements)).astype(F32).astype(BF16)
    cell_hot[:, 0:LANES] = own
    cell_hot[:, LANES : 2 * LANES] = own

    value, rates, halos_one = section_rates(0, fields_ref, vel_ref, mass_ref, drops_first)
    for f in range(6):
        fields_one[NODES * f : NODES * (f + 1), :] = field(value, f) + TIME_STEP * rates[f]
    value, rates, halos_two = section_rates(1, fields_one, vel_one, mass_one, drops_second)
    for f in range(6):
        gas_out[NODES * f : NODES * (f + 1), :] = 0.5 * fields_ref[
            NODES * f : NODES * (f + 1), :
        ] + 0.5 * (field(value, f) + TIME_STEP * rates[f])

    whole(ids_ref, ids_in, ids_sems).wait_send()
    for section in range(2):
        whole(states_out.at[section], states_in.at[section], state_sems.at[section]).wait_send()
        whole(dep_out.at[section], dep_in.at[section], dep_sems.at[section]).wait_send()
    for copy in halos_one + halos_two:
        copy.wait_send()


def lane_split(elements):
    assert elements <= LANES <= 3 * elements
    return (LANES - elements) // 2


def element_of(lane_id, elements):
    extra = lane_split(elements)
    return jnp.where(
        lane_id < elements, lane_id,
        jnp.where(lane_id < elements + extra, lane_id - elements, lane_id - (LANES - elements)),
    )


def on_device(
    density, momentum, energy, fuel_density, drop_pos, drop_vel, drop_mass, block_cell, block_count
):
    n_inner = lax.axis_size("inner")
    fields = jnp.concatenate([density[None], momentum, fuel_density[None], energy[None]], 0)
    elements = fields.shape[3] // 3
    blocks = block_cell.shape[0]
    drops = blocks * PB
    slots = n_inner * CAP
    parcel = 4.0 * elements / drops
    extra = lane_split(elements)

    table = fields.reshape(6, 3, 3, elements, 3).transpose(0, 4, 1, 2, 3).reshape(6, 27, elements)
    table = jnp.concatenate([table, table[:, : NODES - 27]], 1)
    table = jnp.concatenate(
        [table, table[:, :, :extra], table[:, :, 2 * elements + extra - LANES :]], 2
    ).reshape(6 * NODES, LANES)

    owner = block_cell // elements
    earlier = jnp.sum((owner[None, :] < owner[:, None]).astype(jnp.int32), 1)
    slot = owner * CAP + jnp.arange(blocks, dtype=jnp.int32) - earlier
    local = block_cell - owner * elements
    taken = slot[None, :] == jnp.arange(slots, dtype=jnp.int32)[:, None]
    ids = (jnp.sum(jnp.where(taken, local[None, :] + 1, 0), 1) - 1).astype(F32)
    ids = jnp.broadcast_to(ids.reshape(n_inner, CAP, 1), (n_inner, CAP, LANES))
    live = (jnp.arange(PB)[None, :] < block_count[:, None]).astype(F32).reshape(1, drops)
    drop_slot = jnp.repeat(slot.astype(F32), PB).reshape(1, drops)

    vmem = pl.BlockSpec(memory_space=pltpu.VMEM)
    gas, vel, mass = pl.pallas_call(
        functools.partial(gas_kernel, elements, parcel),
        out_shape=(
            jax.ShapeDtypeStruct((6 * NODES, LANES), F32),
            jax.ShapeDtypeStruct((3, drops), F32),
            jax.ShapeDtypeStruct((1, drops), F32),
        ),
        in_specs=[vmem] * 9,
        out_specs=(vmem, vmem, vmem),
        scratch_shapes=[
            pltpu.VMEM((6 * NODES, LANES), F32),
            pltpu.VMEM((6 * NODES, LANES), F32),
            pltpu.VMEM((3 * NODES, 6 * LANES), F32),
            pltpu.VMEM((NODES, drops), F32),
            pltpu.VMEM((2 * slots, drops), BF16),
            pltpu.VMEM((slots, 2 * LANES), BF16),
            pltpu.VMEM((n_inner, CAP, LANES), F32),
            pltpu.VMEM((2, n_inner, CAP, WIDE), F32),
            pltpu.VMEM((2, n_inner, CAP, WIDE), F32),
            pltpu.VMEM((2, n_inner, CAP, WIDE), F32),
            pltpu.VMEM((2, n_inner, CAP, WIDE), F32),
            pltpu.VMEM((2, 2, 6 * NODES, LANES), F32),
            pltpu.VMEM((2, 2, 6 * NODES, LANES), F32),
            pltpu.VMEM((2 * SENT, slots), F32),
            pltpu.VMEM((3, drops), F32),
            pltpu.VMEM((1, drops), F32),
            pltpu.SemaphoreType.DMA((2,)),
            pltpu.SemaphoreType.DMA((2, 2)),
            pltpu.SemaphoreType.DMA((2, 2)),
            pltpu.SemaphoreType.DMA((2, 4)),
            pltpu.SemaphoreType.DMA((2, 4)),
        ],
        compiler_params=pltpu.CompilerParams(
            collective_id=0, has_side_effects=True, vmem_limit_bytes=48 * 1024 * 1024
        ),
    )(
        table, ids, drop_slot, live, drop_pos, drop_vel, drop_mass.reshape(1, drops),
        jnp.asarray(derivative_rows()), jnp.asarray(node_scale()),
    )
    gas = gas.reshape(6, NODES, LANES)[:, :27, :elements].reshape(6, 3, 3, 3, elements)
    gas = gas.transpose(0, 2, 3, 4, 1).reshape(6, 3, 3, 3 * elements)
    gas = jnp.concatenate([gas[:4], gas[5:6], gas[4:5]], 0)
    return gas, vel, mass.reshape(drops)


def solution(mesh):
    placed = (
        P("region", "inner", None),
        P(None, "region", "inner", None),
        P("region", "inner", None),
        P("region", "inner", None),
        P(None, ("region", "inner")),
        P(None, ("region", "inner")),
        P(("region", "inner")),
        P(("region", "inner")),
        P(("region", "inner")),
    )
    return jax.shard_map(
        on_device,
        mesh=mesh,
        in_specs=placed,
        out_specs=(
            P(None, "region", "inner", None),
            P(None, ("region", "inner")),
            P(("region", "inner")),
        ),
        check_vma=False,
    )
```

time: 199 us -> 47.7 us (0.24)
  waiting for transfers between devices: 86.6 us -> 0 us
  blocking collectives: 47 us -> 0 us
  Pallas kernels: 0 us -> 35.9 us
  local copies, waits for them, and re-layouts: 26.8 us -> 9.86 us
  between operations: 15.4 us -> 0.89 us
  matrix products: 11.6 us -> 0 us
  starting transfers between devices: 5.34 us -> 0 us
  other arithmetic: 5.71 us -> 0.65 us
    reduce_scatter x2 -> x0, waiting for transfers between devices: 75.6 us -> none  [return_sources(): lax.psum_scatter(jnp.dot(chosen, deposit_rows, precision=lax.Precision.HI...]
    all_gather x2 -> x0, blocking collectives: 47 us -> none  [fetch_states(): shard_rows = lax.all_gather(rows_table, 'inner', axis=0, tiled=True)]
    pallas_call x0 -> x1, Pallas kernels: none -> 35.9 us  [on_device(): pl.pallas_call(functools.partial(gas_kernel, elements, parcel), out_shape...]
    dot_general x14 -> x0, matrix products: 11.6 us -> none  [the longest x2 3.52 us: droplet_terms(): jnp.einsum('kbp,fbp->bfk', weights, sources, precision=lax.Precision.HIGH...]
    ppermute x8 -> x0, waiting for transfers between devices: 10.9 us -> none  [the longest x4 9.85 us: padded_2(): lax.ppermute(lax.slice_in_dim(block, block.shape[dim] - width, None, axis...]
    reshape x22 -> x0, local copies, waits for them, and re-layouts: 6.37 us -> none  [the longest x2 1.15 us: node_layout(): return rows_table.reshape(elements, 6, 3, 3, 3).transpose(1, 2, 3, 0, 4)....]
    unnamed x26, local copies, waits for them, and re-layouts: 0.76 us -> 6.35 us
    ppermute x8 -> x0, starting transfers between devices: 5.26 us -> none  [the longest x4 3.25 us: padded_2(): lax.ppermute(lax.slice_in_dim(block, 0, width, axis=dim), axis, backward)]
  transfers between devices with their start and end apart: 10 -> 0, of which waited for: 7 -> 0; matrix products, arithmetic and copies ran while one was open for 8% -> 0% of each run, Pallas kernels for 0% -> 0%
where the time goes in v1:
time: 47.7 us; the launch traced here: 47.3 us
  Pallas kernels  35.9 us (75%)
  local copies, waits for them, and re-layouts  9.86 us (21%)
  between operations  0.89 us (2%)
  other arithmetic  0.65 us (1%)
    pallas_call x1, Pallas kernels, on_device(): pl.pallas_call(functools.partial(gas_kernel, elements, parcel), out_shape...  35.9 us
    unnamed x26, local copies, waits for them, and re-layouts  6.35 us
    concatenate x8, local copies, waits for them, and re-layouts, on_device(): jnp.concatenate([density[None], momentum, fuel_density[None], energy[None...  1.55 us
    slice x8, local copies, waits for them, and re-layouts, on_device(): gas = jnp.concatenate([gas[:4], gas[5:6], gas[4:5]], 0)  1.52 us

profile of v1, /device:TPU:0, one launch (start us, length us, event | category | flops | bytes accessed | tf_op | source)
XLA Modules:
  0.0 47.3 jit_solution(255264457586467182)
XLA Ops:
  0.6 0.6 %copy-done.10 = s32[64]{0:T(128)S(1)} copy-done((s32[64]{0:T(128)S(1)}, s32[64]{0:T(128)}, u32[]{:S(2)}) %copy-start.10) | copy-done | bytes 280
  1.3 0.2 convert_reduce_fusion
  1.9 0.6 %copy-done.9 = s32[64]{0:T(128)S(1)} copy-done((s32[64]{0:T(128)S(1)}, s32[64]{0:T(128)}, u32[]{:S(2)}) %copy-start.9) | copy-done | bytes 280
  2.7 0.6 %copy-done.6 = f32[3,3,144]{2,1,0:T(4,128)S(1)} copy-done((f32[3,3,144]{2,1,0:T(4,128)S(1)}, f32[3,3,144]{2,1,0:T(4,128)}, u32[]{:S(2)}) %copy-start.6) | copy-done | bytes 5208
  3.3 0.2 concatenate.21
  3.6 0.6 %copy-done.7 = f32[3,3,144]{2,1,0:T(4,128)S(1)} copy-done((f32[3,3,144]{2,1,0:T(4,128)S(1)}, f32[3,3,144]{2,1,0:T(4,128)}, u32[]{:S(2)}) %copy-start.7) | copy-done | bytes 5208
  4.2 0.2 concatenate.24
  4.5 0.6 %copy-done.8 = f32[3,3,144]{2,1,0:T(4,128)S(1)} copy-done((f32[3,3,144]{2,1,0:T(4,128)S(1)}, f32[3,3,144]{2,1,0:T(4,128)}, u32[]{:S(2)}) %copy-start.8) | copy-done | bytes 5208
  5.1 0.2 concatenate.23
  5.4 0.6 %copy-done.5 = f32[3,3,3,144]{3,2,1,0:T(4,128)S(1)} copy-done((f32[3,3,3,144]{3,2,1,0:T(4,128)S(1)}, f32[3,3,3,144]{3,2,1,0:T(4,128)}, u32[]{:S(2)}) %copy-start.5) | copy-done | bytes 15576
  6.0 0.4 concatenate.22
  6.4 0.3 copy.36
  6.9 0.1 fusion
  7.1 0.7 %copy-done = f32[3,2048]{1,0:T(4,128)S(1)} copy-done((f32[3,2048]{1,0:T(4,128)S(1)}, f32[3,2048]{1,0:T(4,128)}, u32[]{:S(2)}) %copy-start) | copy-done | bytes 24600
  7.8 35.9 %shard_map.130 = (f32[192,128]{1,0:T(8,128)S(1)}, f32[3,2048]{1,0:T(4,128)S(1)}, f32[1,2048]{1,0:T(1,128)S(1)}) custom-call(f32[192,128]{1,0:T(8,128)S(1)} %bitcast.23, f32[16,8,128]{2,1,0:T(8,128)S(1)} %broadcast_in_dim.18.ids_ref, f32[1,2048]{1,0:T(1,128)S(1)} %reshape_reshape.3.slot_ref, f32[1,2048]{1,0:T(1,128)S(1)} %reshape.86.live_ref, ...), custom_call_target="tpu_custom_call" | custom-call | tf_op jit(solution)/shard_map/pallas_call | solution.py:346
  43.8 0.1 copy.43
  44.0 0.2 slice.37
  44.2 0.1 copy.44
  44.4 0.2 slice.39
  44.6 0.4 copy.42
  45.0 0.4 slice.35
  45.4 0.7 %copy.45 = f32[6,3,3,144]{3,2,1,0:T(4,128)} copy(f32[6,3,3,144]{3,0,2,1:T(8,128)S(1)} %pad_maximum_fusion) | data formatting | bytes 62208
  46.1 0.6 %copy.49 = f32[3,2048]{1,0:T(4,128)} copy(f32[3,2048]{1,0:T(4,128)S(1)} %get-tuple-element.31) | data formatting | bytes 49152
  46.7 0.6 %copy.50 = f32[2048]{0:T(1024)} copy(f32[2048]{0:T(1024)S(1)} %bitcast.26) | data formatting | bytes 16384
  (37 shorter events, 1.3 us)
Async XLA Ops:
  0.6 0.7 %copy-start.10 = (s32[64]{0:T(128)S(1)}, s32[64]{0:T(128)}, u32[]{:S(2)}) copy-start(s32[64]{0:T(128)} %param.18) | copy-start | bytes 772
  1.8 0.7 %copy-start.9 = (s32[64]{0:T(128)S(1)}, s32[64]{0:T(128)}, u32[]{:S(2)}) copy-start(s32[64]{0:T(128)} %param.19) | copy-start | bytes 772
  2.6 0.7 %copy-start.6 = (f32[3,3,144]{2,1,0:T(4,128)S(1)}, f32[3,3,144]{2,1,0:T(4,128)}, u32[]{:S(2)}) copy-start(f32[3,3,144]{2,1,0:T(4,128)} %param.11) | copy-start | bytes 15556
  3.5 0.7 %copy-start.7 = (f32[3,3,144]{2,1,0:T(4,128)S(1)}, f32[3,3,144]{2,1,0:T(4,128)}, u32[]{:S(2)}) copy-start(f32[3,3,144]{2,1,0:T(4,128)} %param.13) | copy-start | bytes 15556
  4.4 0.7 %copy-start.8 = (f32[3,3,144]{2,1,0:T(4,128)S(1)}, f32[3,3,144]{2,1,0:T(4,128)}, u32[]{:S(2)}) copy-start(f32[3,3,144]{2,1,0:T(4,128)} %param.14) | copy-start | bytes 15556
  5.3 0.8 %copy-start.5 = (f32[3,3,3,144]{3,2,1,0:T(4,128)S(1)}, f32[3,3,3,144]{3,2,1,0:T(4,128)}, u32[]{:S(2)}) copy-start(f32[3,3,3,144]{3,2,1,0:T(4,128)} %param.12) | copy-start | bytes 46660
  7.0 0.8 %copy-start = (f32[3,2048]{1,0:T(4,128)S(1)}, f32[3,2048]{1,0:T(4,128)}, u32[]{:S(2)}) copy-start(f32[3,2048]{1,0:T(4,128)} %pos_ref.1) | copy-start | bytes 73732
  7.1 0.8 %copy-start.1 = (f32[3,2048]{1,0:T(4,128)S(1)}, f32[3,2048]{1,0:T(4,128)}, u32[]{:S(2)}) copy-start(f32[3,2048]{1,0:T(4,128)} %vel_ref.1) | copy-start | bytes 73732
  7.1 0.8 %copy-start.2 = (f32[32,192]{1,0:T(8,128)S(1)}, f32[32,192]{1,0:T(8,128)}, u32[]{:S(2)}) copy-start(f32[32,192]{1,0:T(8,128)} %constant.22.clone.deriv_ref) | copy-start | bytes 73732
  7.1 0.8 %copy-start.3 = (f32[32,128]{1,0:T(8,128)S(1)}, f32[32,128]{1,0:T(8,128)}, u32[]{:S(2)}) copy-start(f32[32,128]{1,0:T(8,128)} %constant.23.clone.scale_ref) | copy-start | bytes 49156
  7.1 0.8 %copy-start.4 = (f32[2048]{0:T(1024)S(1)}, f32[2048]{0:T(1024)}, u32[]{:S(2)}) copy-start(f32[2048]{0:T(1024)} %param.17) | copy-start | bytes 24580

commit v2 on v1

--- a/solution.py
+++ b/solution.py
@@ -47,6 +47,12 @@
     return high, (value - high.astype(F32)).astype(BF16)
 
 
+def thirds(value):
+    high = value.astype(BF16)
+    rest = value - high.astype(F32)
+    return (high,) + halves(rest)
+
+
 def nt_dot(left, right):
     return lax.dot_general(left, right, (((1,), (1,)), ((), ())), preferred_element_type=F32)
 
@@ -78,10 +84,11 @@
 
 def gas_kernel(
     elements, parcel,
-    fields_ref, ids_ref, slot_ref, live_ref, pos_ref, vel_ref, mass_ref, deriv_ref, scale_ref,
+    density_ref, momentum_ref, energy_ref, fuel_ref, pos_ref, vel_ref, mass_ref, cell_ref,
+    count_ref, deriv_ref, scale_ref,
     gas_out, vel_out, mass_out,
-    fields_one, tend, flux_scr, weights, drop_hot, cell_hot,
-    ids_in, states_out, states_in, dep_out, dep_in, low_in, high_in, dep_acc, vel_one, mass_one,
+    natural, fields_ref, ids_ref, live_ref, pick, fields_one, tend, flux_scr, weights, drop_hot, cell_hot,
+    ids_in, states_out, states_in, dep_out, dep_in, low_in, high_in, dep_acc, vel_one, mass_one, by_lane,
     ids_sems, state_sems, dep_sems, halo_send, halo_recv,
 ):
     n_inner, n_region = lax.axis_size("inner"), lax.axis_size("region")
@@ -106,19 +113,22 @@
     for other in region_peers:
         pl.semaphore_signal(barrier, inc=1, device_id=(other, me), device_id_type=MESH)
 
-    row = lax.broadcasted_iota(jnp.int32, (NODES, drops), 0)
-
-    def basis(d, place):
-        t = pos_ref[d : d + 1, :]
-        first, mid, last = 0.5 * t * (t - 1.0), 1.0 - t * t, 0.5 * t * (t + 1.0)
-        return jnp.where(place == 0, first, jnp.where(place == 1, mid, last))
-
-    product = basis(0, row // 3 % 3) * basis(1, row % 3) * basis(2, row // 9)
-    weights[...] = jnp.where(row < 27, product, 0.0)
-    hot_row = lax.broadcasted_iota(jnp.int32, (slots, drops), 0).astype(F32)
-    hot = (hot_row == slot_ref[0:1, :]).astype(F32).astype(BF16)
-    drop_hot[0:slots, :] = hot
-    drop_hot[slots : 2 * slots, :] = hot
+    blocks = cell_ref.shape[1]
+    cell = cell_ref[...].astype(F32)
+    owner = jnp.floor((cell + 0.5) * (1.0 / elements))
+    local = cell - owner * elements
+    square = (blocks, blocks)
+    across = jnp.broadcast_to(owner, square)
+    diagonal = lax.broadcasted_iota(jnp.int32, square, 0) == lax.broadcasted_iota(
+        jnp.int32, square, 1
+    )
+    down = jnp.sum(jnp.where(diagonal, across, 0.0), 1, keepdims=True)
+    earlier = jnp.sum(jnp.where(down < across, 1.0, 0.0), 0, keepdims=True)
+    rank = lax.broadcasted_iota(jnp.int32, (1, blocks), 1).astype(F32) - earlier
+    slot_of = lax.broadcasted_iota(jnp.int32, (slots, blocks), 0).astype(F32)
+    taken = slot_of == owner * CAP + rank
+    ids = jnp.sum(jnp.where(taken, local + 1.0, 0.0), 1, keepdims=True) - 1.0
+    ids_ref[...] = jnp.broadcast_to(ids, (slots, LANES)).reshape(n_inner, CAP, LANES)
 
     pl.semaphore_wait(barrier, n_inner - 1 + len(region_peers))
 
@@ -142,6 +152,54 @@
 
     exchange(ids_ref, ids_in, ids_sems)
     ids_in[me] = ids_ref[me]
+
+    for x in range(3):
+        for f in range(6):
+            part = (density_ref, momentum_ref, momentum_ref, momentum_ref, fuel_ref, energy_ref)[f]
+            natural[9 * f + 3 * x : 9 * f + 3 * x + 3, :] = (
+                part[f - 1, x] if 1 <= f <= 3 else part[x]
+            )
+    length = 3 * elements
+    node_z = lax.broadcasted_iota(jnp.int32, (length, LANES), 0)
+    pick_lane = lax.broadcasted_iota(jnp.int32, (length, LANES), 1)
+    first_node = 3 * element_of(pick_lane, elements)
+    for c in range(3):
+        chosen = (node_z == first_node + c).astype(F32)
+        pick[:, LANES * c : LANES * (c + 1)] = chosen.astype(BF16)
+    for_lanes = sum(
+        jnp.dot(part, pick[...], preferred_element_type=F32) for part in thirds(natural[...])
+    )
+    for c in range(3):
+        for f in range(6):
+            rows = for_lanes[9 * f : 9 * f + 9, LANES * c : LANES * (c + 1)]
+            fields_ref[NODES * f + 9 * c : NODES * f + 9 * c + 9, :] = rows
+            if c == 0:
+                fields_ref[NODES * f + 27 : NODES * (f + 1), :] = rows[0 : NODES - 27]
+
+    row = lax.broadcasted_iota(jnp.int32, (NODES, drops), 0)
+
+    def basis(d, place):
+        t = pos_ref[d : d + 1, :]
+        first, mid, last = 0.5 * t * (t - 1.0), 1.0 - t * t, 0.5 * t * (t + 1.0)
+        return jnp.where(place == 0, first, jnp.where(place == 1, mid, last))
+
+    product = basis(0, row // 3 % 3) * basis(1, row % 3) * basis(2, row // 9)
+    weights[...] = jnp.where(row < 27, product, 0.0)
+    in_block = lax.broadcasted_iota(jnp.int32, (blocks, drops), 1) // PB
+    block_row = lax.broadcasted_iota(jnp.int32, (blocks, drops), 0)
+    which = lax.broadcasted_iota(jnp.int32, (16, blocks), 0)
+    wanted = jnp.where(
+        which == 0, owner, jnp.where(which == 1, rank, count_ref[...].astype(F32))
+    ).astype(BF16)
+    spread = jnp.dot(
+        wanted, (in_block == block_row).astype(F32).astype(BF16), preferred_element_type=F32
+    )
+    turn = (lax.broadcasted_iota(jnp.int32, (1, drops), 1) % PB).astype(F32)
+    live_ref[...] = jnp.where(turn < spread[2:3], 1.0, 0.0)
+    hot_row = lax.broadcasted_iota(jnp.int32, (slots, drops), 0).astype(F32)
+    hot = (hot_row == spread[0:1] * CAP + spread[1:2]).astype(F32).astype(BF16)
+    drop_hot[0:slots, :] = hot
+    drop_hot[slots : 2 * slots, :] = hot
 
     lane = lax.broadcasted_iota(jnp.int32, (SENT, LANES), 1)
     node = lax.broadcasted_iota(jnp.int32, (6 * NODES, LANES), 0) % NODES
@@ -288,10 +346,17 @@
     for f in range(6):
         fields_one[NODES * f : NODES * (f + 1), :] = field(value, f) + TIME_STEP * rates[f]
     value, rates, halos_two = section_rates(1, fields_one, vel_one, mass_one, drops_second)
+    own_lane = lax.broadcasted_iota(jnp.int32, (NODES, LANES), 1) < elements
     for f in range(6):
-        gas_out[NODES * f : NODES * (f + 1), :] = 0.5 * fields_ref[
-            NODES * f : NODES * (f + 1), :
-        ] + 0.5 * (field(value, f) + TIME_STEP * rates[f])
+        whole_rows = slice(NODES * f, NODES * (f + 1))
+        final = 0.5 * fields_ref[whole_rows, :] + 0.5 * (field(value, f) + TIME_STEP * rates[f])
+        final = jnp.where(own_lane, final, 0.0)
+        for c in range(3):
+            by_lane[9 * f : 9 * f + 9, LANES * c : LANES * (c + 1)] = final[9 * c : 9 * c + 9]
+    grid = sum(nt_dot(part, pick[...]) for part in thirds(by_lane[...]))
+    for f, target in enumerate((0, 1, 2, 3, 5, 4)):
+        for x in range(3):
+            gas_out[target, x] = grid[9 * f + 3 * x : 9 * f + 3 * x + 3]
 
     whole(ids_ref, ids_in, ids_sems).wait_send()
     for section in range(2):
@@ -318,41 +383,28 @@
     density, momentum, energy, fuel_density, drop_pos, drop_vel, drop_mass, block_cell, block_count
 ):
     n_inner = lax.axis_size("inner")
-    fields = jnp.concatenate([density[None], momentum, fuel_density[None], energy[None]], 0)
-    elements = fields.shape[3] // 3
+    elements = density.shape[2] // 3
     blocks = block_cell.shape[0]
     drops = blocks * PB
     slots = n_inner * CAP
     parcel = 4.0 * elements / drops
-    extra = lane_split(elements)
-
-    table = fields.reshape(6, 3, 3, elements, 3).transpose(0, 4, 1, 2, 3).reshape(6, 27, elements)
-    table = jnp.concatenate([table, table[:, : NODES - 27]], 1)
-    table = jnp.concatenate(
-        [table, table[:, :, :extra], table[:, :, 2 * elements + extra - LANES :]], 2
-    ).reshape(6 * NODES, LANES)
-
-    owner = block_cell // elements
-    earlier = jnp.sum((owner[None, :] < owner[:, None]).astype(jnp.int32), 1)
-    slot = owner * CAP + jnp.arange(blocks, dtype=jnp.int32) - earlier
-    local = block_cell - owner * elements
-    taken = slot[None, :] == jnp.arange(slots, dtype=jnp.int32)[:, None]
-    ids = (jnp.sum(jnp.where(taken, local[None, :] + 1, 0), 1) - 1).astype(F32)
-    ids = jnp.broadcast_to(ids.reshape(n_inner, CAP, 1), (n_inner, CAP, LANES))
-    live = (jnp.arange(PB)[None, :] < block_count[:, None]).astype(F32).reshape(1, drops)
-    drop_slot = jnp.repeat(slot.astype(F32), PB).reshape(1, drops)
 
     vmem = pl.BlockSpec(memory_space=pltpu.VMEM)
     gas, vel, mass = pl.pallas_call(
         functools.partial(gas_kernel, elements, parcel),
         out_shape=(
-            jax.ShapeDtypeStruct((6 * NODES, LANES), F32),
+            jax.ShapeDtypeStruct((6, 3, 3, 3 * elements), F32),
             jax.ShapeDtypeStruct((3, drops), F32),
             jax.ShapeDtypeStruct((1, drops), F32),
         ),
-        in_specs=[vmem] * 9,
+        in_specs=[vmem] * 11,
         out_specs=(vmem, vmem, vmem),
         scratch_shapes=[
+            pltpu.VMEM((54, 3 * elements), F32),
+            pltpu.VMEM((6 * NODES, LANES), F32),
+            pltpu.VMEM((n_inner, CAP, LANES), F32),
+            pltpu.VMEM((1, drops), F32),
+            pltpu.VMEM((3 * elements, 3 * LANES), BF16),
             pltpu.VMEM((6 * NODES, LANES), F32),
             pltpu.VMEM((6 * NODES, LANES), F32),
             pltpu.VMEM((3 * NODES, 6 * LANES), F32),
@@ -369,6 +421,7 @@
             pltpu.VMEM((2 * SENT, slots), F32),
             pltpu.VMEM((3, drops), F32),
             pltpu.VMEM((1, drops), F32),
+            pltpu.VMEM((54, 3 * LANES), F32),
             pltpu.SemaphoreType.DMA((2,)),
             pltpu.SemaphoreType.DMA((2, 2)),
             pltpu.SemaphoreType.DMA((2, 2)),
@@ -379,12 +432,10 @@
             collective_id=0, has_side_effects=True, vmem_limit_bytes=48 * 1024 * 1024
         ),
     )(
-        table, ids, drop_slot, live, drop_pos, drop_vel, drop_mass.reshape(1, drops),
+        density, momentum, energy, fuel_density, drop_pos, drop_vel, drop_mass.reshape(1, drops),
+        block_cell.reshape(1, blocks), block_count.reshape(1, blocks),
         jnp.asarray(derivative_rows()), jnp.asarray(node_scale()),
     )
-    gas = gas.reshape(6, NODES, LANES)[:, :27, :elements].reshape(6, 3, 3, 3, elements)
-    gas = gas.transpose(0, 2, 3, 4, 1).reshape(6, 3, 3, 3 * elements)
-    gas = jnp.concatenate([gas[:4], gas[5:6], gas[4:5]], 0)
     return gas, vel, mass.reshape(drops)
 
 

time: 47.7 us -> 46.5 us (0.975)
  local copies, waits for them, and re-layouts: 9.86 us -> 9.08 us
  other arithmetic: 0.65 us -> 0 us
    unnamed x26 -> x25, local copies, waits for them, and re-layouts: 6.35 us -> 9.08 us
    concatenate x9 -> x0, local copies, waits for them, and re-layouts: 1.57 us -> none  [the longest x8 1.55 us: on_device(): jnp.concatenate([density[None], momentum, fuel_density[None], energy[None...]
    slice x9 -> x0, local copies, waits for them, and re-layouts: 1.53 us -> none  [the longest x8 1.52 us: on_device(): gas = jnp.concatenate([gas[:4], gas[5:6], gas[4:5]], 0)]
where the time goes in v2:
time: 46.5 us; the launch traced here: 45.8 us
  Pallas kernels  36.1 us (78%)
  local copies, waits for them, and re-layouts  9.08 us (20%)
  between operations  0.67 us (1%)
    pallas_call x1, Pallas kernels, on_device(): pl.pallas_call(functools.partial(gas_kernel, elements, parcel), out_shape...  36.1 us
    unnamed x25, local copies, waits for them, and re-layouts  9.08 us

profile of v2, /device:TPU:0, one launch (start us, length us, event | category | flops | bytes accessed | tf_op | source)
XLA Modules:
  0.0 45.8 jit_solution(4644793218841081857)
XLA Ops:
  0.6 0.0 copy-start.9
  0.6 0.0 copy-start.10
  0.7 0.6 %copy-done.9 = s32[64]{0:T(128)S(1)} copy-done((s32[64]{0:T(128)S(1)}, s32[64]{0:T(128)}, u32[]{:S(2)}) %copy-start.9) | copy-done | bytes 280
  1.3 0.0 copy-done.10
  1.3 0.0 copy-start
  1.3 0.8 %copy-done = f32[3,3,3,144]{3,2,1,0:T(4,128)S(1)} copy-done((f32[3,3,3,144]{3,2,1,0:T(4,128)S(1)}, f32[3,3,3,144]{3,2,1,0:T(4,128)}, u32[]{:S(2)}) %copy-start) | copy-done | bytes 15576
  2.1 0.0 copy-start.1
  2.1 0.8 %copy-done.1 = f32[3,2048]{1,0:T(4,128)S(1)} copy-done((f32[3,2048]{1,0:T(4,128)S(1)}, f32[3,2048]{1,0:T(4,128)}, u32[]{:S(2)}) %copy-start.1) | copy-done | bytes 24600
  2.8 0.0 copy-start.2
  2.8 0.8 %copy-done.2 = f32[3,2048]{1,0:T(4,128)S(1)} copy-done((f32[3,2048]{1,0:T(4,128)S(1)}, f32[3,2048]{1,0:T(4,128)}, u32[]{:S(2)}) %copy-start.2) | copy-done | bytes 24600
  3.6 0.0 copy-start.3
  3.6 0.8 %copy-done.3 = f32[32,192]{1,0:T(8,128)S(1)} copy-done((f32[32,192]{1,0:T(8,128)S(1)}, f32[32,192]{1,0:T(8,128)}, u32[]{:S(2)}) %copy-start.3) | copy-done | bytes 24600
  4.3 0.0 copy-start.4
  4.4 0.7 %copy-done.4 = f32[32,128]{1,0:T(8,128)S(1)} copy-done((f32[32,128]{1,0:T(8,128)S(1)}, f32[32,128]{1,0:T(8,128)}, u32[]{:S(2)}) %copy-start.4) | copy-done | bytes 16408
  5.1 0.0 copy-start.5
  5.1 0.7 %copy-done.5 = f32[3,3,144]{2,1,0:T(4,128)S(1)} copy-done((f32[3,3,144]{2,1,0:T(4,128)S(1)}, f32[3,3,144]{2,1,0:T(4,128)}, u32[]{:S(2)}) %copy-start.5) | copy-done | bytes 5208
  5.8 0.0 copy-start.6
  5.8 0.7 %copy-done.6 = f32[3,3,144]{2,1,0:T(4,128)S(1)} copy-done((f32[3,3,144]{2,1,0:T(4,128)S(1)}, f32[3,3,144]{2,1,0:T(4,128)}, u32[]{:S(2)}) %copy-start.6) | copy-done | bytes 5208
  6.5 0.7 %copy-done.7 = f32[3,3,144]{2,1,0:T(4,128)S(1)} copy-done((f32[3,3,144]{2,1,0:T(4,128)S(1)}, f32[3,3,144]{2,1,0:T(4,128)}, u32[]{:S(2)}) %copy-start.7) | copy-done | bytes 5208
  7.2 0.7 %copy-done.8 = f32[2048]{0:T(1024)S(1)} copy-done((f32[2048]{0:T(1024)S(1)}, f32[2048]{0:T(1024)}, u32[]{:S(2)}) %copy-start.8) | copy-done | bytes 8216
  7.9 36.1 %shard_map.130 = (f32[6,3,3,144]{3,2,1,0:T(4,128)S(1)}, f32[3,2048]{1,0:T(4,128)S(1)}, f32[1,2048]{1,0:T(1,128)S(1)}) custom-call(f32[3,3,144]{2,1,0:T(4,128)S(1)} %copy-done.5, f32[3,3,3,144]{3,2,1,0:T(4,128)S(1)} %copy-done, f32[3,3,144]{2,1,0:T(4,128)S(1)} %copy-done.6, f32[3,3,144]{2,1,0:T(4,128)S(1)} %copy-done.7, f32[3,2048]{1,0:T(4,128)S(1)} %copy-done.1, ...), custom_call_target="tpu_custom_call" | custom-call | tf_op jit(solution)/shard_map/pallas_call | solution.py:393
  44.0 0.6 %copy.17 = f32[6,3,3,144]{3,2,1,0:T(4,128)} copy(f32[6,3,3,144]{3,2,1,0:T(4,128)S(1)} %get-tuple-element.12) | data formatting | bytes 62208
  44.6 0.6 %copy.18 = f32[3,2048]{1,0:T(4,128)} copy(f32[3,2048]{1,0:T(4,128)S(1)} %get-tuple-element.13) | data formatting | bytes 49152
  45.2 0.6 %copy.19 = f32[2048]{0:T(1024)} copy(f32[2048]{0:T(1024)S(1)} %bitcast.5) | data formatting | bytes 16384
  (2 shorter events, 0.0 us)
Async XLA Ops:
  0.6 0.7 %copy-start.9 = (s32[64]{0:T(128)S(1)}, s32[64]{0:T(128)}, u32[]{:S(2)}) copy-start(s32[64]{0:T(128)} %param.18) | copy-start | bytes 772
  0.6 0.7 %copy-start.10 = (s32[64]{0:T(128)S(1)}, s32[64]{0:T(128)}, u32[]{:S(2)}) copy-start(s32[64]{0:T(128)} %param.19) | copy-start | bytes 772
  1.3 0.8 %copy-start = (f32[3,3,3,144]{3,2,1,0:T(4,128)S(1)}, f32[3,3,3,144]{3,2,1,0:T(4,128)}, u32[]{:S(2)}) copy-start(f32[3,3,3,144]{3,2,1,0:T(4,128)} %momentum_ref.1) | copy-start | bytes 46660
  2.1 0.8 %copy-start.1 = (f32[3,2048]{1,0:T(4,128)S(1)}, f32[3,2048]{1,0:T(4,128)}, u32[]{:S(2)}) copy-start(f32[3,2048]{1,0:T(4,128)} %pos_ref.1) | copy-start | bytes 73732
  2.8 0.8 %copy-start.2 = (f32[3,2048]{1,0:T(4,128)S(1)}, f32[3,2048]{1,0:T(4,128)}, u32[]{:S(2)}) copy-start(f32[3,2048]{1,0:T(4,128)} %vel_ref.1) | copy-start | bytes 73732
  3.6 0.8 %copy-start.3 = (f32[32,192]{1,0:T(8,128)S(1)}, f32[32,192]{1,0:T(8,128)}, u32[]{:S(2)}) copy-start(f32[32,192]{1,0:T(8,128)} %constant.4.clone.deriv_ref) | copy-start | bytes 73732
  4.3 0.7 %copy-start.4 = (f32[32,128]{1,0:T(8,128)S(1)}, f32[32,128]{1,0:T(8,128)}, u32[]{:S(2)}) copy-start(f32[32,128]{1,0:T(8,128)} %constant.5.clone.scale_ref) | copy-start | bytes 49156
  5.1 0.7 %copy-start.5 = (f32[3,3,144]{2,1,0:T(4,128)S(1)}, f32[3,3,144]{2,1,0:T(4,128)}, u32[]{:S(2)}) copy-start(f32[3,3,144]{2,1,0:T(4,128)} %density_ref.1) | copy-start | bytes 15556
  5.8 0.7 %copy-start.6 = (f32[3,3,144]{2,1,0:T(4,128)S(1)}, f32[3,3,144]{2,1,0:T(4,128)}, u32[]{:S(2)}) copy-start(f32[3,3,144]{2,1,0:T(4,128)} %energy_ref.1) | copy-start | bytes 15556
  6.5 0.7 %copy-start.7 = (f32[3,3,144]{2,1,0:T(4,128)S(1)}, f32[3,3,144]{2,1,0:T(4,128)}, u32[]{:S(2)}) copy-start(f32[3,3,144]{2,1,0:T(4,128)} %fuel_ref.1) | copy-start | bytes 15556
  7.2 0.7 %copy-start.8 = (f32[2048]{0:T(1024)S(1)}, f32[2048]{0:T(1024)}, u32[]{:S(2)}) copy-start(f32[2048]{0:T(1024)} %param.17) | copy-start | bytes 24580

commit v3 on v2

v3 whole, which is shorter than its diff:
```python
import functools

import jax
import jax.numpy as jnp
import numpy as np
from jax import lax
from jax.experimental import pallas as pl
from jax.experimental.pallas import tpu as pltpu
from jax.sharding import PartitionSpec as P

PB = 32
CAP = 8
GAMMA = 1.4
TIME_STEP = 0.05
EVAP_RATE = 0.5
LATENT = 0.5
LANES = 128
PER_LINE = LANES // PB
NODES = 32
SENT = 5 * NODES
WIDE = 256
STRIDES = (3, 1, 9)
F32, BF16 = jnp.float32, jnp.bfloat16
MESH = pl.DeviceIdType.MESH


def derivative_rows():
    line = np.array([[-1.5, 2.0, -0.5], [-0.5, 0.0, 0.5], [0.5, -2.0, 1.5]])
    table = np.zeros((NODES, 3 * NODES))
    for node in range(27):
        for d, stride in enumerate(STRIDES):
            place = node // stride % 3
            for j in range(3):
                table[node, d * NODES + node + (j - place) * stride] = -line[place, j]
    return np.concatenate([table, table], 1).astype(np.float32)


def node_scale():
    q = np.array([1.0 / 3.0, 4.0 / 3.0, 1.0 / 3.0])
    table = np.zeros((NODES, LANES), np.float32)
    for node in range(27):
        table[node] = 1.0 / (q[node // 3 % 3] * q[node % 3] * q[node // 9])
    return table


def halves(value):
    high = value.astype(BF16)
    return high, (value - high.astype(F32)).astype(BF16)


def thirds(value):
    high = value.astype(BF16)
    rest = value - high.astype(F32)
    return (high,) + halves(rest)


def nt_dot(left, right):
    return lax.dot_general(left, right, (((1,), (1,)), ((), ())), preferred_element_type=F32)


def field(value, f):
    return value[NODES * f : NODES * (f + 1)]


def flux_parts(value):
    inverse = 1.0 / field(value, 0)
    speeds = [field(value, 1 + c) * inverse for c in range(3)]
    kinetic = sum(field(value, 1 + c) * speeds[c] for c in range(3))
    pressure = (GAMMA - 1.0) * (field(value, 5) - 0.5 * kinetic)
    sound = jnp.sqrt(GAMMA * pressure * inverse)
    return speeds, pressure, sound


def flux_rows(value, parts, d):
    speeds, pressure, _ = parts
    speed = speeds[d]
    rows = [field(value, 1 + d)]
    for c in range(3):
        row = field(value, 1 + c) * speed
        rows.append(row + pressure if c == d else row)
    rows.append(field(value, 4) * speed)
    rows.append((field(value, 5) + pressure) * speed)
    return rows


def gas_kernel(
    elements, parcel,
    density_hbm, momentum_hbm, energy_hbm, fuel_hbm, pos_hbm, vel_hbm, mass_hbm, deriv_hbm,
    scale_hbm, cell_ref,
    gas_out, vel_out, mass_out,
    density_ref, momentum_ref, energy_ref, fuel_ref, pos_ref, vel_ref, mass_ref, deriv_ref,
    scale_ref,
    natural, fields_ref, pick, fields_one, tend, flux_scr, lines, packed, weights, gathered,
    deposits, drops_out, drops_in, back_out, back_in, low_in, high_in, by_lane, placed_out,
    in_sems, out_sems, back_sems, halo_send, halo_recv,
):
    n_inner, n_region = lax.axis_size("inner"), lax.axis_size("region")
    me, my_region = lax.axis_index("inner"), lax.axis_index("region")
    slots = n_inner * CAP
    blocks = cell_ref.shape[1]
    lines_n = blocks // PER_LINE
    inner_low, inner_high = lax.rem(me + n_inner - 1, n_inner), lax.rem(me + 1, n_inner)
    region_low = lax.rem(my_region + n_region - 1, n_region)
    region_high = lax.rem(my_region + 1, n_region)

    loads = [
        pltpu.make_async_copy(src, dst, in_sems.at[n])
        for n, (src, dst) in enumerate((
            (pos_hbm, pos_ref), (vel_hbm, vel_ref), (mass_hbm, mass_ref),
            (density_hbm, density_ref), (momentum_hbm, momentum_ref), (energy_hbm, energy_ref),
            (fuel_hbm, fuel_ref), (deriv_hbm, deriv_ref), (scale_hbm, scale_ref),
        ))
    ]
    for load in loads:
        load.start()

    bits = [1 << n for n in range((n_inner - 1).bit_length())]
    paired = n_inner == 1 << len(bits)

    def peer_of(j):
        if not paired:
            return lax.rem(me + j, n_inner)
        return sum((me // b % 2 + j // b % 2) % 2 * b for b in bits)

    def each_peer(body):
        if n_inner <= 16:
            for j in range(n_inner - 1, 0, -1):
                body(peer_of(j))
        else:
            @pl.loop(1, n_inner)
            def _(j):
                body(peer_of(n_inner - j))

    barrier = pltpu.get_barrier_semaphore()

    def greet(peer):
        pl.semaphore_signal(barrier, inc=1, device_id=(my_region, peer), device_id_type=MESH)

    each_peer(greet)
    region_peers = [region_high] if n_region == 2 else [region_low, region_high]
    for other in region_peers:
        pl.semaphore_signal(barrier, inc=1, device_id=(other, me), device_id_type=MESH)

    cell = cell_ref[0:1, :].astype(F32)
    owner = jnp.floor((cell + 0.5) * (1.0 / elements))
    local = cell - owner * elements
    square = (blocks, blocks)
    diagonal = lax.broadcasted_iota(jnp.int32, square, 0) == lax.broadcasted_iota(
        jnp.int32, square, 1
    )

    def upright(row):
        return jnp.sum(
            jnp.where(diagonal, jnp.broadcast_to(row, square), 0.0), 1, keepdims=True
        )

    down = upright(owner)
    earlier = jnp.sum(jnp.where(down < jnp.broadcast_to(owner, square), 1.0, 0.0), 0, keepdims=True)
    lane_b = lax.broadcasted_iota(jnp.int32, (1, blocks), 1)
    number = (lane_b % lines_n * PER_LINE + lane_b // lines_n).astype(F32)
    slot = owner * CAP + number - earlier
    taken = lax.broadcasted_iota(jnp.int32, (slots, blocks), 0).astype(F32) == slot
    taken = taken.astype(F32).astype(BF16)
    taken_up = lax.broadcasted_iota(jnp.int32, (blocks, slots), 1).astype(F32) == upright(slot)
    taken_up = taken_up.astype(F32).astype(BF16)

    for load in loads[:3]:
        load.wait()
    for q in range(7):
        src = (pos_ref, vel_ref, mass_ref)[q // 3]
        for r in range(lines_n):
            lines[q, r : r + 1, :] = src[q % 3 : q % 3 + 1, LANES * r : LANES * (r + 1)]
    for q in range(7):
        for j in range(PER_LINE):
            packed[lines_n * j : lines_n * (j + 1), PB * q : PB * (q + 1)] = lines[
                q, :, PB * j : PB * (j + 1)
            ]
    turn = lax.broadcasted_iota(jnp.int32, (blocks, PB), 1).astype(F32)
    mark = upright(local) + 1.0
    count = upright(cell_ref[1:2, :].astype(F32))
    packed[:, 7 * PB : 8 * PB] = jnp.where(turn < count, mark, -mark)
    by_slot = sum(
        jnp.dot(taken, part, preferred_element_type=F32) for part in thirds(packed[...])
    )
    drops_out[...] = by_slot.reshape(n_inner, CAP, WIDE)

    pl.semaphore_wait(barrier, n_inner - 1 + len(region_peers))

    def exchange(src, dst, sems):
        def send(peer):
            pltpu.make_async_remote_copy(
                src_ref=src.at[peer], dst_ref=dst.at[me],
                send_sem=sems.at[0], recv_sem=sems.at[1],
                device_id=(my_region, peer), device_id_type=MESH,
            ).start()

        each_peer(send)
        dst[me] = src[me]

    def whole(src, dst, sems):
        part = pl.ds(0, n_inner - 1)
        return pltpu.make_async_remote_copy(
            src_ref=src.at[part], dst_ref=dst.at[part],
            send_sem=sems.at[0], recv_sem=sems.at[1],
            device_id=(my_region, inner_high), device_id_type=MESH,
        )

    exchange(drops_out, drops_in, out_sems)
    for load in loads[3:]:
        load.wait()

    for x in range(3):
        for f in range(6):
            part = (density_ref, momentum_ref, momentum_ref, momentum_ref, fuel_ref, energy_ref)[f]
            natural[9 * f + 3 * x : 9 * f + 3 * x + 3, :] = (
                part[f - 1, x] if 1 <= f <= 3 else part[x]
            )
    length = 3 * elements
    node_z = lax.broadcasted_iota(jnp.int32, (length, LANES), 0)
    pick_lane = lax.broadcasted_iota(jnp.int32, (length, LANES), 1)
    first_node = 3 * element_of(pick_lane, elements)
    for c in range(3):
        chosen = (node_z == first_node + c).astype(F32)
        pick[:, LANES * c : LANES * (c + 1)] = chosen.astype(BF16)
    for_lanes = sum(
        jnp.dot(part, pick[...], preferred_element_type=F32) for part in thirds(natural[...])
    )
    for c in range(3):
        for f in range(6):
            rows = for_lanes[9 * f : 9 * f + 9, LANES * c : LANES * (c + 1)]
            fields_ref[NODES * f + 9 * c : NODES * f + 9 * c + 9, :] = rows
            if c == 0:
                fields_ref[NODES * f + 27 : NODES * (f + 1), :] = rows[0 : NODES - 27]

    node = lax.broadcasted_iota(jnp.int32, (6 * NODES, LANES), 0) % NODES

    def halo_copies(section, src):
        copies = [
            (src, high_in.at[section, 1], 0, (my_region, inner_low)),
            (src, low_in.at[section, 1], 1, (my_region, inner_high)),
            (src, high_in.at[section, 0], 2, (region_low, me)),
        ]
        if n_region != 2:
            copies.append((src, low_in.at[section, 0], 3, (region_high, me)))
        return [
            pltpu.make_async_remote_copy(
                src_ref=a, dst_ref=b, send_sem=halo_send.at[section, i],
                recv_sem=halo_recv.at[section, i], device_id=dev, device_id_type=MESH,
            )
            for a, b, i, dev in copies
        ]

    def lifts(value, parts, low, high, d):
        stride = STRIDES[d]
        place = node // stride % 3
        first, last = (place == 0) & (node < 27), (place == 2) & (node < 27)
        rows = 6 * NODES
        beyond = jnp.where(
            first, pltpu.roll(low, rows - 2 * stride, 0),
            jnp.where(last, pltpu.roll(high, 2 * stride, 0), value),
        )
        other = flux_parts(beyond)
        wave = 1.5 * jnp.maximum(
            jnp.abs(parts[0][d]) + parts[2], jnp.abs(other[0][d]) + other[2]
        )
        sign = jnp.where(first, 1.5, -1.5)[0:NODES]
        here, there = flux_rows(value, parts, d), flux_rows(beyond, other, d)
        return [
            sign * (there[f] - here[f]) + wave * (field(beyond, f) - field(value, f))
            for f in range(6)
        ]

    def local_fluid(value, parts):
        for d in range(3):
            for f, part in enumerate(flux_rows(value, parts, d)):
                flux_scr[NODES * d : NODES * (d + 1), LANES * f : LANES * (f + 1)] = part
        volume = jnp.dot(
            deriv_ref[...].astype(BF16), jnp.concatenate(halves(flux_scr[...]), 0),
            preferred_element_type=F32,
        )
        along = lifts(value, parts, pltpu.roll(value, 1, 1), pltpu.roll(value, LANES - 1, 1), 2)
        for f in range(6):
            tend[NODES * f : NODES * (f + 1), :] = (
                volume[:, LANES * f : LANES * (f + 1)] + along[f]
            )

    def face_fluid(section, value, parts, halos):
        for copy in halos:
            copy.wait_recv()
        low_x = high_in[section, 0] if n_region == 2 else low_in[section, 0]
        along_x = lifts(value, parts, low_x, high_in[section, 0], 0)
        along_y = lifts(value, parts, low_in[section, 1], high_in[section, 1], 1)
        for f in range(6):
            tend[NODES * f : NODES * (f + 1), :] += along_x[f] + along_y[f]

    halos_one = halo_copies(0, fields_ref)
    for copy in halos_one:
        copy.start()
    value = fields_ref[...]
    parts = flux_parts(value)
    local_fluid(value, parts)
    face_fluid(0, value, parts, halos_one)
    deposits[...] = jnp.zeros_like(deposits)

    whole(drops_out, drops_in, out_sems).wait_recv()
    arrived = drops_in[...].reshape(slots, WIDE).T
    pos = [arrived[PB * q : PB * (q + 1)] for q in range(3)]
    vel = [arrived[PB * (3 + q) : PB * (4 + q)] for q in range(3)]
    mark = arrived[7 * PB : 8 * PB]
    live = jnp.where(mark > 0.0, 1.0, 0.0)
    mass = jnp.where(mark == 0.0, 1.0, arrived[6 * PB : 7 * PB])
    place = jnp.maximum(jnp.abs(mark[0:1]) - 1.0, 0.0)
    hot_lane = lax.broadcasted_iota(jnp.int32, (LANES, slots), 0).astype(F32)
    hot = element_of(hot_lane, elements) == place
    hot = hot.astype(F32).astype(BF16)
    basis = [(0.5 * t * (t - 1.0), 1.0 - t * t, 0.5 * t * (t + 1.0)) for t in pos]
    for c in range(3):
        for a in range(3):
            pair = basis[0][a] * basis[2][c]
            for b in range(3):
                at = PB * (9 * c + 3 * a + b)
                weights[at : at + PB, :] = pair * basis[1][b]
    lane = lax.broadcasted_iota(jnp.int32, (SENT, LANES), 1)

    def drop_section(value, vel, mass):
        held = jnp.where(lane < elements, value[0:SENT], 0.0)
        gathered[...] = sum(
            jnp.dot(part, hot, preferred_element_type=F32) for part in thirds(held)
        )
        gas = [0.0] * 5
        for k in range(27):
            w = weights[PB * k : PB * (k + 1), :]
            for f in range(5):
                gas[f] = gas[f] + gathered[NODES * f + k : NODES * f + k + 1, :] * w
        inverse = 1.0 / gas[0]
        rel = [gas[1 + c] * inverse - vel[c] for c in range(3)]
        cube_root = jnp.exp(jnp.log(mass) * (1.0 / 3.0))
        drag = live / (cube_root * cube_root)
        accel = [drag * rel[c] for c in range(3)]
        evap = (
            live * EVAP_RATE * cube_root
            * jnp.sqrt(1.0 + (rel[0] * rel[0] + rel[1] * rel[1] + rel[2] * rel[2]))
            * (1.0 - gas[4] * inverse)
        )
        force = [mass * accel[c] for c in range(3)]
        work = sum(force[c] * vel[c] for c in range(3))
        speed_two = sum(vel[c] * vel[c] for c in range(3))
        sources = [evap] + [evap * vel[c] - force[c] for c in range(3)]
        sources.append(evap * (LATENT + 0.5 * speed_two) - work)
        return accel, evap, sources

    def deposit(sources):
        for k in range(27):
            w = weights[PB * k : PB * (k + 1), :]
            for f in range(5):
                deposits[NODES * f + k : NODES * f + k + 1, :] = jnp.sum(
                    w * sources[f], 0, keepdims=True
                )
        summed = sum(nt_dot(part, hot) for part in halves(deposits[...]))
        scale = scale_ref[...] * parcel
        return [scale * field(summed, source) for source in (0, 1, 2, 3, 0, 4)]

    accel, evap, sources = drop_section(value, vel, mass)
    added = deposit(sources)
    for f in range(6):
        rows = slice(NODES * f, NODES * (f + 1))
        fields_one[rows, :] = field(value, f) + TIME_STEP * (tend[rows, :] + added[f])
    halos_two = halo_copies(1, fields_one)
    for copy in halos_two:
        copy.start()
    vel_one = [vel[c] + TIME_STEP * accel[c] for c in range(3)]
    mass_one = mass - TIME_STEP * evap
    value = fields_one[...]
    accel, evap, sources = drop_section(value, vel_one, mass_one)
    final = [0.5 * vel[c] + 0.5 * (vel_one[c] + TIME_STEP * accel[c]) for c in range(3)]
    final.append(0.5 * mass + 0.5 * (mass_one - TIME_STEP * evap))
    back_out[...] = jnp.concatenate(final, 0).T.reshape(n_inner, CAP, LANES)
    exchange(back_out, back_in, back_sems)

    parts = flux_parts(value)
    local_fluid(value, parts)
    added = deposit(sources)
    face_fluid(1, value, parts, halos_two)
    own_lane = lax.broadcasted_iota(jnp.int32, (NODES, LANES), 1) < elements
    for f in range(6):
        rows = slice(NODES * f, NODES * (f + 1))
        ended = 0.5 * fields_ref[rows, :] + 0.5 * (
            field(value, f) + TIME_STEP * (tend[rows, :] + added[f])
        )
        ended = jnp.where(own_lane, ended, 0.0)
        for c in range(3):
            by_lane[9 * f : 9 * f + 9, LANES * c : LANES * (c + 1)] = ended[9 * c : 9 * c + 9]
    grid = sum(nt_dot(part, pick[...]) for part in thirds(by_lane[...]))
    for f, target in enumerate((0, 1, 2, 3, 5, 4)):
        for x in range(3):
            gas_out[target, x] = grid[9 * f + 3 * x : 9 * f + 3 * x + 3]

    whole(back_out, back_in, back_sems).wait_recv()
    came = back_in[...].reshape(slots, LANES)
    by_block = sum(jnp.dot(taken_up, part, preferred_element_type=F32) for part in thirds(came))
    for q in range(4):
        for j in range(PER_LINE):
            placed_out[q, :, PB * j : PB * (j + 1)] = by_block[
                lines_n * j : lines_n * (j + 1), PB * q : PB * (q + 1)
            ]
    for q in range(4):
        for r in range(lines_n):
            dst = mass_out if q == 3 else vel_out
            dst[q % 3 : q % 3 + 1, LANES * r : LANES * (r + 1)] = placed_out[q, r : r + 1, :]

    whole(drops_out, drops_in, out_sems).wait_send()
    whole(back_out, back_in, back_sems).wait_send()
    for copy in halos_one + halos_two:
        copy.wait_send()


def lane_split(elements):
    assert elements <= LANES <= 3 * elements
    return (LANES - elements) // 2


def element_of(lane_id, elements):
    extra = lane_split(elements)
    return jnp.where(
        lane_id < elements, lane_id,
        jnp.where(lane_id < elements + extra, lane_id - elements, lane_id - (LANES - elements)),
    )


def on_device(
    density, momentum, energy, fuel_density, drop_pos, drop_vel, drop_mass, block_cell, block_count
):
    n_inner = lax.axis_size("inner")
    elements = density.shape[2] // 3
    blocks = block_cell.shape[0]
    drops = blocks * PB
    slots = n_inner * CAP
    parcel = 4.0 * elements / drops

    cells = jnp.stack([block_cell, block_count]).reshape(2, blocks // PER_LINE, PER_LINE)
    cells = cells.transpose(0, 2, 1).reshape(2, blocks)

    vmem = pl.BlockSpec(memory_space=pltpu.VMEM)
    hbm = pl.BlockSpec(memory_space=pltpu.HBM)
    loaded = (
        density, momentum, energy, fuel_density, drop_pos, drop_vel, drop_mass.reshape(1, drops),
        jnp.asarray(derivative_rows()), jnp.asarray(node_scale()),
    )
    lines_n = blocks // PER_LINE
    gas, vel, mass = pl.pallas_call(
        functools.partial(gas_kernel, elements, parcel),
        out_shape=(
            jax.ShapeDtypeStruct((6, 3, 3, 3 * elements), F32),
            jax.ShapeDtypeStruct((3, drops), F32),
            jax.ShapeDtypeStruct((1, drops), F32),
        ),
        in_specs=[hbm] * len(loaded) + [vmem],
        out_specs=(vmem, vmem, vmem),
        scratch_shapes=[pltpu.VMEM(x.shape, F32) for x in loaded] + [
            pltpu.VMEM((54, 3 * elements), F32),
            pltpu.VMEM((6 * NODES, LANES), F32),
            pltpu.VMEM((3 * elements, 3 * LANES), BF16),
            pltpu.VMEM((6 * NODES, LANES), F32),
            pltpu.VMEM((6 * NODES, LANES), F32),
            pltpu.VMEM((3 * NODES, 6 * LANES), F32),
            pltpu.VMEM((7, lines_n, LANES), F32),
            pltpu.VMEM((blocks, WIDE), F32),
            pltpu.VMEM((27 * PB, slots), F32),
            pltpu.VMEM((SENT, slots), F32),
            pltpu.VMEM((SENT, slots), F32),
            pltpu.VMEM((n_inner, CAP, WIDE), F32),
            pltpu.VMEM((n_inner, CAP, WIDE), F32),
            pltpu.VMEM((n_inner, CAP, LANES), F32),
            pltpu.VMEM((n_inner, CAP, LANES), F32),
            pltpu.VMEM((2, 2, 6 * NODES, LANES), F32),
            pltpu.VMEM((2, 2, 6 * NODES, LANES), F32),
            pltpu.VMEM((54, 3 * LANES), F32),
            pltpu.VMEM((4, lines_n, LANES), F32),
            pltpu.SemaphoreType.DMA((len(loaded),)),
            pltpu.SemaphoreType.DMA((2,)),
            pltpu.SemaphoreType.DMA((2,)),
            pltpu.SemaphoreType.DMA((2, 4)),
            pltpu.SemaphoreType.DMA((2, 4)),
        ],
        compiler_params=pltpu.CompilerParams(
            collective_id=0, has_side_effects=True, vmem_limit_bytes=62 * 1024 * 1024
        ),
    )(*loaded, cells)
    return gas, vel, mass.reshape(drops)


def solution(mesh):
    placed = (
        P("region", "inner", None),
        P(None, "region", "inner", None),
        P("region", "inner", None),
        P("region", "inner", None),
        P(None, ("region", "inner")),
        P(None, ("region", "inner")),
        P(("region", "inner")),
        P(("region", "inner")),
        P(("region", "inner")),
    )
    return jax.shard_map(
        on_device,
        mesh=mesh,
        in_specs=placed,
        out_specs=(
            P(None, "region", "inner", None),
            P(None, ("region", "inner")),
            P(("region", "inner")),
        ),
        check_vma=False,
    )
```

time: 46.5 us -> 26 us (0.56)
  Pallas kernels: 36.1 us -> 20 us
  local copies, waits for them, and re-layouts: 9.08 us -> 5.06 us
    pallas_call x1, Pallas kernels: 36.1 us -> 20 us  [on_device(): pl.pallas_call(functools.partial(gas_kernel, elements, parcel), out_shape...]
    unnamed x25 -> x11, local copies, waits for them, and re-layouts: 9.08 us -> 4.07 us
    reshape x0 -> x1, local copies, waits for them, and re-layouts: none -> 0.66 us  [on_device(): cells = cells.transpose(0, 2, 1).reshape(2, blocks)]
where the time goes in v3:
time: 26 us; the launch traced here: 25.7 us
  Pallas kernels  20 us (77%)
  local copies, waits for them, and re-layouts  5.06 us (19%)
  between operations  0.67 us (3%)
    pallas_call x1, Pallas kernels, on_device(): pl.pallas_call(functools.partial(gas_kernel, elements, parcel), out_shape...  20 us
    unnamed x11, local copies, waits for them, and re-layouts  4.07 us
    reshape x1, local copies, waits for them, and re-layouts, on_device(): cells = cells.transpose(0, 2, 1).reshape(2, blocks)  0.66 us

profile of v3, /device:TPU:0, one launch (start us, length us, event | category | flops | bytes accessed | tf_op | source)
XLA Modules:
  0.0 25.7 jit_solution(14019198398395817971)
XLA Ops:
  0.6 0.0 copy-start.2
  0.6 0.6 %copy-done.2 = s32[64]{0:T(128)S(1)} copy-done((s32[64]{0:T(128)S(1)}, s32[64]{0:T(128)}, u32[]{:S(2)}) %copy-start.2) | copy-done | bytes 280
  1.3 0.1 stack.9
  1.4 0.0 copy-start.3
  1.4 0.1 copy.16
  1.5 0.6 %copy-done.3 = s32[64]{0:T(128)S(1)} copy-done((s32[64]{0:T(128)S(1)}, s32[64]{0:T(128)}, u32[]{:S(2)}) %copy-start.3) | copy-done | bytes 280
  2.0 0.1 stack.10
  2.1 0.1 copy.17
  2.2 0.7 %reshape.21.cell_ref = s32[2,64]{1,0:T(2,128)} reshape(s32[2,4,16]{2,1,0:T(4,128)S(1)} %add_bitcast_fusion) | data formatting | bytes 1024 | tf_op jit(solution)/shard_map/reshape | solution.py:441
  2.9 20.0 %shard_map.130 = (f32[6,3,3,144]{3,2,1,0:T(4,128)}, f32[3,2048]{1,0:T(4,128)}, f32[1,2048]{1,0:T(1,128)}) custom-call(f32[3,3,144]{2,1,0:T(4,128)} %density_hbm.1, f32[3,3,3,144]{3,2,1,0:T(4,128)} %momentum_hbm.1, f32[3,3,144]{2,1,0:T(4,128)} %energy_hbm.1, f32[3,3,144]{2,1,0:T(4,128)} %fuel_hbm.1, f32[3,2048]{1,0:T(4,128)} %pos_hbm.1, f32[3,2048]{1,0:T(4,128)} %vel_hbm.1, ...), custom_call_target="tpu_custom_call" | custom-call | tf_op jit(solution)/shard_map/pallas_call | solution.py:450
  22.9 0.0 copy-start
  22.9 1.5 %copy.21 = f32[6,3,3,144]{3,2,1,0:T(4,128)} copy(f32[6,3,3,144]{3,2,1,0:T(4,128)} %get-tuple-element.12) | data formatting | bytes 62208
  24.4 0.0 copy-done
  24.4 0.0 copy-start.1
  24.4 0.6 %copy.22 = f32[3,2048]{1,0:T(4,128)} copy(f32[3,2048]{1,0:T(4,128)S(1)} %copy-done) | data formatting | bytes 49152
  25.0 0.1 copy-done.1
  25.1 0.6 %copy.23 = f32[2048]{0:T(1024)} copy(f32[2048]{0:T(1024)S(1)} %bitcast.5) | data formatting | bytes 16384
  (1 shorter events, 0.0 us)
Async XLA Ops:
  0.6 0.7 %copy-start.2 = (s32[64]{0:T(128)S(1)}, s32[64]{0:T(128)}, u32[]{:S(2)}) copy-start(s32[64]{0:T(128)} %param.18) | copy-start | bytes 772
  1.4 0.7 %copy-start.3 = (s32[64]{0:T(128)S(1)}, s32[64]{0:T(128)}, u32[]{:S(2)}) copy-start(s32[64]{0:T(128)} %param.19) | copy-start | bytes 772
  22.9 1.5 %copy-start = (f32[3,2048]{1,0:T(4,128)S(1)}, f32[3,2048]{1,0:T(4,128)}, u32[]{:S(2)}) copy-start(f32[3,2048]{1,0:T(4,128)} %get-tuple-element.13) | copy-start | bytes 73732
  24.4 0.7 %copy-start.1 = (f32[1,2048]{1,0:T(1,128)S(1)}, f32[1,2048]{1,0:T(1,128)}, u32[]{:S(2)}) copy-start(f32[1,2048]{1,0:T(1,128)} %get-tuple-element.8) | copy-start | bytes 24580

commit v4 on v3

--- a/solution.py
+++ b/solution.py
@@ -86,10 +86,10 @@
 def gas_kernel(
     elements, parcel,
     density_hbm, momentum_hbm, energy_hbm, fuel_hbm, pos_hbm, vel_hbm, mass_hbm, deriv_hbm,
-    scale_hbm, cell_ref,
+    scale_hbm, cell_hbm, count_hbm,
     gas_out, vel_out, mass_out,
     density_ref, momentum_ref, energy_ref, fuel_ref, pos_ref, vel_ref, mass_ref, deriv_ref,
-    scale_ref,
+    scale_ref, cell_ref, count_ref,
     natural, fields_ref, pick, fields_one, tend, flux_scr, lines, packed, weights, gathered,
     deposits, drops_out, drops_in, back_out, back_in, low_in, high_in, by_lane, placed_out,
     in_sems, out_sems, back_sems, halo_send, halo_recv,
@@ -109,9 +109,10 @@
             (pos_hbm, pos_ref), (vel_hbm, vel_ref), (mass_hbm, mass_ref),
             (density_hbm, density_ref), (momentum_hbm, momentum_ref), (energy_hbm, energy_ref),
             (fuel_hbm, fuel_ref), (deriv_hbm, deriv_ref), (scale_hbm, scale_ref),
+            (cell_hbm, cell_ref), (count_hbm, count_ref),
         ))
     ]
-    for load in loads:
+    for load in loads[9:] + loads[:9]:
         load.start()
 
     bits = [1 << n for n in range((n_inner - 1).bit_length())]
@@ -141,7 +142,16 @@
     for other in region_peers:
         pl.semaphore_signal(barrier, inc=1, device_id=(other, me), device_id_type=MESH)
 
-    cell = cell_ref[0:1, :].astype(F32)
+    for load in loads[9:]:
+        load.wait()
+    lane_b = lax.broadcasted_iota(jnp.int32, (blocks, blocks), 1)
+    block_at = lane_b % lines_n * PER_LINE + lane_b // lines_n
+    moved = block_at == lax.broadcasted_iota(jnp.int32, (blocks, blocks), 0)
+    moved = moved.astype(F32).astype(BF16)
+    both = lax.broadcasted_iota(jnp.int32, (16, blocks), 0) == 0
+    both = jnp.where(both, cell_ref[...], count_ref[...]).astype(F32)
+    both = sum(jnp.dot(part, moved, preferred_element_type=F32) for part in halves(both))
+    cell = both[0:1]
     owner = jnp.floor((cell + 0.5) * (1.0 / elements))
     local = cell - owner * elements
     square = (blocks, blocks)
@@ -177,7 +187,7 @@
             ]
     turn = lax.broadcasted_iota(jnp.int32, (blocks, PB), 1).astype(F32)
     mark = upright(local) + 1.0
-    count = upright(cell_ref[1:2, :].astype(F32))
+    count = upright(both[1:2])
     packed[:, 7 * PB : 8 * PB] = jnp.where(turn < count, mark, -mark)
     by_slot = sum(
         jnp.dot(taken, part, preferred_element_type=F32) for part in thirds(packed[...])
@@ -206,7 +216,7 @@
         )
 
     exchange(drops_out, drops_in, out_sems)
-    for load in loads[3:]:
+    for load in loads[3:9]:
         load.wait()
 
     for x in range(3):
@@ -437,14 +447,12 @@
     slots = n_inner * CAP
     parcel = 4.0 * elements / drops
 
-    cells = jnp.stack([block_cell, block_count]).reshape(2, blocks // PER_LINE, PER_LINE)
-    cells = cells.transpose(0, 2, 1).reshape(2, blocks)
-
     vmem = pl.BlockSpec(memory_space=pltpu.VMEM)
     hbm = pl.BlockSpec(memory_space=pltpu.HBM)
     loaded = (
         density, momentum, energy, fuel_density, drop_pos, drop_vel, drop_mass.reshape(1, drops),
         jnp.asarray(derivative_rows()), jnp.asarray(node_scale()),
+        block_cell.reshape(1, blocks), block_count.reshape(1, blocks),
     )
     lines_n = blocks // PER_LINE
     gas, vel, mass = pl.pallas_call(
@@ -454,9 +462,9 @@
             jax.ShapeDtypeStruct((3, drops), F32),
             jax.ShapeDtypeStruct((1, drops), F32),
         ),
-        in_specs=[hbm] * len(loaded) + [vmem],
+        in_specs=[hbm] * len(loaded),
         out_specs=(vmem, vmem, vmem),
-        scratch_shapes=[pltpu.VMEM(x.shape, F32) for x in loaded] + [
+        scratch_shapes=[pltpu.VMEM(x.shape, x.dtype) for x in loaded] + [
             pltpu.VMEM((54, 3 * elements), F32),
             pltpu.VMEM((6 * NODES, LANES), F32),
             pltpu.VMEM((3 * elements, 3 * LANES), BF16),
@@ -485,7 +493,7 @@
         compiler_params=pltpu.CompilerParams(
             collective_id=0, has_side_effects=True, vmem_limit_bytes=62 * 1024 * 1024
         ),
-    )(*loaded, cells)
+    )(*loaded)
     return gas, vel, mass.reshape(drops)
 
 

time: 26 us -> 23.4 us (0.90)
  local copies, waits for them, and re-layouts: 5.06 us -> 2.85 us
  Pallas kernels: 20 us -> 19.6 us
    unnamed x11 -> x7, local copies, waits for them, and re-layouts: 4.07 us -> 2.85 us
    reshape x1 -> x0, local copies, waits for them, and re-layouts: 0.66 us -> none  [on_device(): cells = cells.transpose(0, 2, 1).reshape(2, blocks)]
    pallas_call x1, Pallas kernels: 20 us -> 19.6 us  [on_device(): pl.pallas_call(functools.partial(gas_kernel, elements, parcel), out_shape...]
    another operation x4 -> x0, local copies, waits for them, and re-layouts: 0.32 us -> none  [on_device(): jnp.stack([block_cell, block_count])]
where the time goes in v4:
time: 23.4 us; the launch traced here: 23.1 us
  Pallas kernels  19.6 us (84%)
  local copies, waits for them, and re-layouts  2.85 us (12%)
  between operations  0.65 us (3%)
    pallas_call x1, Pallas kernels, on_device(): pl.pallas_call(functools.partial(gas_kernel, elements, parcel), out_shape...  19.6 us
    unnamed x7, local copies, waits for them, and re-layouts  2.85 us

profile of v4, /device:TPU:0, one launch (start us, length us, event | category | flops | bytes accessed | tf_op | source)
XLA Modules:
  0.0 23.1 jit_solution(3984164992849437487)
XLA Ops:
  0.6 19.6 %shard_map.130 = (f32[6,3,3,144]{3,2,1,0:T(4,128)}, f32[3,2048]{1,0:T(4,128)}, f32[1,2048]{1,0:T(1,128)}) custom-call(f32[3,3,144]{2,1,0:T(4,128)} %density_hbm.1, f32[3,3,3,144]{3,2,1,0:T(4,128)} %momentum_hbm.1, f32[3,3,144]{2,1,0:T(4,128)} %energy_hbm.1, f32[3,3,144]{2,1,0:T(4,128)} %fuel_hbm.1, f32[3,2048]{1,0:T(4,128)} %pos_hbm.1, f32[3,2048]{1,0:T(4,128)} %vel_hbm.1, ...), custom_call_target="tpu_custom_call" | custom-call | tf_op jit(solution)/shard_map/pallas_call | solution.py:458
  20.3 0.0 copy-start
  20.3 1.5 %copy.17 = f32[6,3,3,144]{3,2,1,0:T(4,128)} copy(f32[6,3,3,144]{3,2,1,0:T(4,128)} %get-tuple-element.12) | data formatting | bytes 62208
  21.8 0.0 copy-done
  21.8 0.0 copy-start.1
  21.8 0.6 %copy.18 = f32[3,2048]{1,0:T(4,128)} copy(f32[3,2048]{1,0:T(4,128)S(1)} %copy-done) | data formatting | bytes 49152
  22.4 0.1 copy-done.1
  22.5 0.6 %copy.19 = f32[2048]{0:T(1024)} copy(f32[2048]{0:T(1024)S(1)} %bitcast.5) | data formatting | bytes 16384
Async XLA Ops:
  20.3 1.5 %copy-start = (f32[3,2048]{1,0:T(4,128)S(1)}, f32[3,2048]{1,0:T(4,128)}, u32[]{:S(2)}) copy-start(f32[3,2048]{1,0:T(4,128)} %get-tuple-element.13) | copy-start | bytes 73732
  21.8 0.7 %copy-start.1 = (f32[1,2048]{1,0:T(1,128)S(1)}, f32[1,2048]{1,0:T(1,128)}, u32[]{:S(2)}) copy-start(f32[1,2048]{1,0:T(1,128)} %get-tuple-element.8) | copy-start | bytes 24580
